TPU v7x, 256 devices: a whole 4x4x8 slice. The times are simulated.
256 devices in a mesh: ctx: 64 (over x_hi, y, z), head: 4 (over x_lo, core).
Axes of the slice: x: 4 (x_hi: 2, x_lo: 2; x = x_hi * 2 + x_lo), y: 4, z: 8, core: 2. Of those that a mesh axis runs over, the one named last changes fastest.
Arguments:
- queries: bfloat16 [8192, 4096], P('ctx', 'head'), may hold values from -9 to 9
- keys: bfloat16 [8192, 512], P('ctx', 'head'), may hold values from -9 to 9
- values: bfloat16 [8192, 512], P('ctx', 'head'), may hold values from -6 to 6
- doc_lengths: int32 [8], replicated, may hold values from 1 to 2048, 8192 in all
- source_row: int32 [64, 128], replicated, may hold values from 0 to 8191, as said below
Outputs:
- attn_out: bfloat16 [8192, 4096], P('ctx', 'head')
- max_logits: float32 [32, 8], replicated
Inputs may be any that keep to these rules, and one draw needn't show every extreme that they name: source_row[d, c * 2 + s] lies in c * 128 .. (c + 1) * 128 - 1 for every d, every c in 0 .. 63 and s in 0 .. 1; every row 0 .. 8191 appears exactly once.
All inputs are finite; a program needn't handle non-finite values.
Results may differ from a plain program's by a relative error of at most 0.007.
Values may be sent and summed in bfloat16 or wider, within the bound.
No kernel may reach another device: no remote copies, remote signals or barrier semaphores. Data moves between devices by JAX's collectives and lax.ppermute only.
A program may use at most 64 MiB of HBM per device.

v0:
```python
import math

import jax
import jax.numpy as jnp
from jax import lax
from jax.sharding import PartitionSpec as P

HD = 128


NEG_BIG = -1e30


def doc_index(positions, doc_ends):
    return jnp.sum((positions[:, None] >= doc_ends[None, :]).astype(jnp.int32), axis=1)


def block_update(
    state_now, queries_grouped, query_pos, query_docs, key_rows, value_rows, key_pos, doc_ends
):
    kv_heads = queries_grouped.shape[1]
    key_count = key_rows.shape[0]
    key_docs = doc_index(key_pos, doc_ends)
    allowed = (query_docs[:, None] == key_docs[None, :]) & (key_pos[None, :] <= query_pos[:, None])
    old_max, row_total, accumulator = state_now
    key_heads = key_rows.reshape(key_count, kv_heads, HD)
    value_heads = value_rows.reshape(key_count, kv_heads, HD)
    scores = jnp.einsum(
        "tkgd,jkd->tkgj", queries_grouped, key_heads, preferred_element_type=jnp.float32
    ) * (1.0 / math.sqrt(HD))
    live_mask = allowed[:, None, None, :]
    scores = jnp.where(live_mask, scores, NEG_BIG)
    new_max = jnp.maximum(old_max, jnp.max(scores, axis=3))
    factor = jnp.exp(old_max - new_max)
    weights = jnp.where(live_mask, jnp.exp(scores - new_max[..., None]), 0.0)
    row_total = row_total * factor + jnp.sum(weights, axis=3)
    accumulator = accumulator * factor[..., None] + jnp.einsum(
        "tkgj,jkd->tkgd",
        weights.astype(jnp.bfloat16),
        value_heads,
        preferred_element_type=jnp.float32,
    )
    return (new_max, row_total, accumulator)


def gather_for_moved(fold_piece, initial, key_rows, value_rows):
    return fold_piece(
        initial,
        (
            lax.all_gather(key_rows, "ctx", axis=0, tiled=True),
            lax.all_gather(value_rows, "ctx", axis=0, tiled=True),
        ),
        jnp.int32(0),
    )


def attend(query_rows, query_pos, key_rows, value_rows, key_pos_of, doc_ends, collect):
    row_count = query_rows.shape[0]
    kv_heads = key_rows.shape[1] // HD
    group_size = query_rows.shape[1] // (kv_heads * HD)
    queries_grouped = query_rows.reshape(row_count, kv_heads, group_size, HD)
    query_docs = doc_index(query_pos, doc_ends)
    initial = (
        jnp.full((row_count, kv_heads, group_size), NEG_BIG, jnp.float32),
        jnp.zeros((row_count, kv_heads, group_size), jnp.float32),
        jnp.zeros((row_count, kv_heads, group_size, HD), jnp.float32),
    )

    def fold_piece(state_now, key_piece, first_row):
        piece_keys, piece_values = key_piece
        key_count = piece_keys.shape[0]
        piece_pos = key_pos_of(first_row, key_count)
        block_len = 512
        block_count = key_count // block_len

        def one_block(block_no, old_state):
            offset = block_no * block_len
            return block_update(
                old_state,
                queries_grouped,
                query_pos,
                query_docs,
                lax.dynamic_slice_in_dim(piece_keys, offset, block_len, 0),
                lax.dynamic_slice_in_dim(piece_values, offset, block_len, 0),
                lax.dynamic_slice_in_dim(piece_pos, offset, block_len, 0),
                doc_ends,
            )

        return lax.fori_loop(0, block_count, one_block, state_now)

    row_max, row_total, accumulator = collect(fold_piece, initial, key_rows, value_rows)
    context = (accumulator / row_total[..., None]).reshape(row_count, -1).astype(jnp.bfloat16)
    return (context, row_max.reshape(row_count, -1), query_docs)


def body(queries, keys, values, doc_lengths, source_row):
    cycle_size = lax.axis_size("ctx")
    my_index = lax.axis_index("ctx")
    row_count = queries.shape[0]
    per_peer = row_count // cycle_size
    doc_ends = jnp.cumsum(doc_lengths)
    send_rows = (
        lax.dynamic_slice_in_dim(source_row, my_index * per_peer, per_peer, 1)
        - my_index * row_count
    ).reshape(-1)
    slot_positions = lax.dynamic_slice_in_dim(source_row, my_index, 1, 0).reshape(-1)
    flat_rows = source_row.reshape(-1)

    def outgoing(tensor):
        return jnp.take(tensor, send_rows, axis=0).reshape(cycle_size, per_peer, tensor.shape[1])

    def moved_key_pos(first_row, key_count):
        return flat_rows

    received = (
        lax.all_to_all(outgoing(queries), "ctx", split_axis=0, concat_axis=0, tiled=True),
        lax.all_to_all(outgoing(keys), "ctx", split_axis=0, concat_axis=0, tiled=True),
        lax.all_to_all(outgoing(values), "ctx", split_axis=0, concat_axis=0, tiled=True),
    )
    local_queries, local_keys, local_values = [tensor.reshape(row_count, -1) for tensor in received]
    context, row_max, query_docs = attend(
        local_queries,
        slot_positions,
        local_keys,
        local_values,
        moved_key_pos,
        doc_ends,
        gather_for_moved,
    )
    doc_hit = query_docs[:, None] == jnp.arange(doc_lengths.shape[0], dtype=jnp.int32)[None, :]
    local_max = jnp.max(jnp.where(doc_hit[:, None, :], row_max[:, :, None], NEG_BIG), axis=0)
    reduced = lax.pmax(local_max, "ctx")
    all_maxima = lax.all_gather(reduced, "head", axis=0, tiled=True)
    return (context, all_maxima)


def solution(mesh):
    return jax.shard_map(
        body,
        mesh=mesh,
        in_specs=(P("ctx", "head"), P("ctx", "head"), P("ctx", "head"), P(), P()),
        out_specs=(P("ctx", "head"), P()),
        check_vma=False,
    )
```

profile of v0, /device:TPU:1, one launch (start us, length us, event | category | flops | bytes accessed | tf_op | source)
XLA Modules:
  0.0 537.7 jit_solution(5748463240690586384)
XLA Ops:
  8.5 1.4 gather_fusion.1
  9.9 1.4 gather_fusion.2
  11.4 25.9 %all_to_all.15 = bf16[64,2,128]{2,1,0:T(2,128)(2,1)} all-to-all(bf16[64,2,128]{2,1,0:T(2,128)(2,1)S(1)} %bitcast.93), channel_id=1, replica_groups=mesh['ctx'=64,'head'=4] {'ctx'}, dimensions={0} | all-to-all | bytes 65536 | tf_op jit(solution)/shard_map/all_to_all | solution.py:117
  37.4 15.3 %all_to_all.16 = bf16[64,2,128]{2,1,0:T(2,128)(2,1)} all-to-all(bf16[64,2,128]{2,1,0:T(2,128)(2,1)S(1)} %bitcast.92), channel_id=1, replica_groups=mesh['ctx'=64,'head'=4] {'ctx'}, dimensions={0} | all-to-all | bytes 65536 | tf_op jit(solution)/shard_map/all_to_all | solution.py:118
  55.0 4.6 all-to-all-start.1
  61.4 10.8 %all-to-all-done.1 = bf16[64,2,1024]{2,1,0:T(2,128)(2,1)S(1)} async-done(((bf16[64,2,1024]{2,1,0:T(2,128)(2,1)}), bf16[64,2,1024]{2,1,0:T(2,128)(2,1)S(1)}, u32[]{:S(2)}, u32[]{:S(2)}) %all-to-all-start.1) | async-done | bytes 262176 | tf_op jit(solution)/shard_map/all_to_all | solution.py:116
  72.4 74.2 %all-gather.3.cloned.1.call-done = bf16[8192,128]{1,0:T(8,128)(2,1)} async-done(((bf16[128,128]{1,0:T(8,128)(2,1)}), bf16[8192,128]{1,0:T(8,128)(2,1)}) %all-gather.3.cloned.1.call-update) | async-done | bytes 2097168 | tf_op jit(solution)/shard_map/all_gather | solution.py:50
  146.6 119.0 %all-gather.5.cloned.1.call-done = bf16[8192,128]{1,0:T(8,128)(2,1)} async-done(((bf16[128,128]{1,0:T(8,128)(2,1)}), bf16[8192,128]{1,0:T(8,128)(2,1)}) %all-gather.5.cloned.1.call-update) | async-done | bytes 2097168 | tf_op jit(solution)/shard_map/all_gather | solution.py:51
  265.6 74.5 %while.18 = (s32[]{:T(128)}, f32[128,1,8]{0,2,1:T(8,128)S(1)}, f32[128,1,8]{0,2,1:T(8,128)S(1)}, f32[128,1,8,128]{0,3,2,1:T(8,128)S(1)}, s32[128]{0:T(128)S(1)},...) while((s32[]{:T(128)}, f32[128,1,8]{0,2,1:T(8,128)S(1)}, ...), condition=%wide.region_6.8_spmd.clone, body=%wide.region_2.0_spmd.clone.sunk | while | flops 275858944 | bytes 8205555 | solution.py:89
  266.6 1.4 fusion.33
  268.0 1.6 fusion.36
  272.7 1.6 fusion.36
  276.0 1.4 fusion.33
  277.4 1.6 fusion.36
  280.6 1.4 fusion.33
  282.0 1.6 fusion.36
  285.3 1.4 fusion.33
  286.7 1.6 fusion.36
  291.3 1.6 fusion.36
  296.0 1.6 fusion.36
  300.6 1.6 fusion.36
  305.3 1.6 fusion.36
  310.0 1.6 fusion.36
  314.6 1.6 fusion.36
  317.9 1.4 fusion.33
  319.3 1.6 fusion.36
  323.9 1.6 fusion.36
  328.6 1.6 fusion.36
  333.2 1.6 fusion.36
  337.9 1.6 fusion.36
  341.1 152.4 %pmax.7 = f32[8,8]{1,0:T(8,128)S(1)} all-reduce(f32[8,8]{1,0:T(8,128)S(1)} %select_reduce_fusion), channel_id=1, replica_groups=mesh['ctx'=64,'head'=4] {'ctx'}, use_global_device_ids=true, to_apply=%region_8.10 | all-reduce | flops 64 | bytes 512 | tf_op jit(solution)/shard_map/pmax | solution.py:132
  493.4 36.8 %all_gather.11 = f32[32,8]{1,0:T(8,128)S(1)} all-gather(f32[8,8]{1,0:T(8,128)S(1)} %pmax.7), channel_id=1, replica_groups=mesh['ctx'=64,'head'=4] {'head'}, dimensions={0}, use_global_device_ids=true | all-gather | bytes 1280 | tf_op jit(solution)/shard_map/all_gather | solution.py:133
  (161 shorter events, 47.7 us)
Async XLA Ops:
  7.2 45.7 %copy-start = (bf16[128,1024]{1,0:T(8,128)(2,1)S(1)}, bf16[128,1024]{1,0:T(8,128)(2,1)}, u32[]{:S(2)}) copy-start(bf16[128,1024]{1,0:T(8,128)(2,1)} %param.9) | copy-start | bytes 786436
  7.2 139.4 %all-gather.3.cloned.1.call-start = ((), (), s32[]{:S(2)}) async-start(), calls=%async_computation.3 | async-start | bytes 2129920 | tf_op jit(solution)/shard_map/all_gather | solution.py:50
  11.4 48.3 %copy-start.1 = (s32[8]{0:T(128)S(1)}, s32[8]{0:T(128)}, u32[]{:S(2)}) copy-start(s32[8]{0:T(128)} %param.12) | copy-start | bytes 100
  37.3 228.3 %all-gather.5.cloned.1.call-start = ((), (), s32[]{:S(2)}) async-start(), calls=%async_computation.4 | async-start | bytes 2129920 | tf_op jit(solution)/shard_map/all_gather | solution.py:51
  55.0 17.2 %all-to-all-start.1 = ((bf16[64,2,1024]{2,1,0:T(2,128)(2,1)}), bf16[64,2,1024]{2,1,0:T(2,128)(2,1)S(1)}, u32[]{:S(2)}, u32[]{:S(2)}) async-start(bf16[64,2,1024]{2,1,0:T(2,128)(2,1)} %broadcast_select_fusion), calls=%async_computation.1 | async-start | bytes 524288 | tf_op jit(solution)/shard_map/all_to_all | solution.py:116
Sparse Core Ops, SparseCore 0:
  37.4 109.1 all-gather.2
  150.1 115.4 all-gather.4
where the time goes:
time: 539 us; the launch traced here: 538 us
  blocking collectives  230 us (43%)
  waiting for transfers between devices  204 us (38%)
  matrix products  47.9 us (9%)
  local copies, waits for them, and re-layouts  20.6 us (4%)
  other arithmetic  14.8 us (3%)
  between operations  14.2 us (3%)
    pmax x1, blocking collectives, body(): reduced = lax.pmax(local_max, 'ctx')  152 us
    all_gather x1, waiting for transfers between devices, gather_for_moved(): lax.all_gather(value_rows, 'ctx', axis=0, tiled=True)  119 us
    all_gather x1, waiting for transfers between devices, gather_for_moved(): lax.all_gather(key_rows, 'ctx', axis=0, tiled=True)  74.2 us
    all_gather x1, blocking collectives, body(): all_maxima = lax.all_gather(reduced, 'head', axis=0, tiled=True)  36.8 us
    dot_general x16, matrix products, block_update(): jnp.einsum('tkgj,jkd->tkgd', weights.astype(jnp.bfloat16), value_heads, p...  26 us
    all_to_all x1, blocking collectives, body(): lax.all_to_all(outgoing(keys), 'ctx', split_axis=0, concat_axis=0, tiled=...  25.9 us
    dot_general x16, matrix products, block_update(): jnp.einsum('tkgd,jkd->tkgj', queries_grouped, key_heads, preferred_elemen...  21.9 us
    all_to_all x1, blocking collectives, body(): lax.all_to_all(outgoing(values), 'ctx', split_axis=0, concat_axis=0, tile...  15.3 us
  transfers between devices with their start and end apart: 3, of which 3 were waited for; matrix products, arithmetic and copies ran while one was open for 1% of the time, Pallas kernels for 0%

commit v1 on v0

v1 whole, which is shorter than its diff:
```python
import functools
import math

import jax
import jax.numpy as jnp
from jax import lax
from jax.experimental import pallas as pl
from jax.experimental.pallas import tpu as pltpu
from jax.sharding import PartitionSpec as P

HD = 128
HEADS = 8
DOCS = 8
ROWS = 128
GROUP = 16
CTX = 64
NEG_BIG = -1e30
SCALE = 1.0 / math.sqrt(HD)
SCALE_LOG2E = SCALE * math.log2(math.e)
HEADS_AT_ONCE = 2


def dot_nt(a, b):
    return lax.dot_general(a, b, (((1,), (1,)), ((), ())), preferred_element_type=jnp.float32)


def attend_kernel(lengths_ref, source_ref, q_ref, kv_ref, own_ref, out_ref, bias_ref, q_scr):
    me = lax.axis_index("ctx")
    lane = lax.broadcasted_iota(jnp.int32, (ROWS, 128), 1)
    row = lax.broadcasted_iota(jnp.int32, (ROWS, 128), 0)
    chunk_lane = lax.broadcasted_iota(jnp.int32, (CTX, 128), 1) // 2
    local = (source_ref[...] - chunk_lane * ROWS).astype(jnp.float32).astype(jnp.bfloat16)
    spread = (
        lax.broadcasted_iota(jnp.int32, (ROWS, CTX), 0) // 2
        == lax.broadcasted_iota(jnp.int32, (ROWS, CTX), 1)
    ).astype(jnp.float32).astype(jnp.bfloat16)
    table = jnp.dot(spread, local, preferred_element_type=jnp.float32)
    wanted = lane == 2 * me + row % 2
    pick = jnp.sum(jnp.where(wanted, table, 0.0), axis=1, keepdims=True).astype(jnp.int32)
    one_hot = (lane == pick).astype(jnp.float32).astype(jnp.bfloat16)
    q_all = jnp.dot(one_hot, q_ref[...], preferred_element_type=jnp.float32)
    for h in range(HEADS):
        q_scr[h * ROWS : (h + 1) * ROWS, :] = q_all[:, h * HD : (h + 1) * HD].astype(jnp.bfloat16)

    pos = me * ROWS + pick
    start = jnp.zeros_like(pos)
    doc = jnp.zeros_like(pos)
    end = jnp.int32(0)
    for i in range(DOCS):
        end = end + lengths_ref[i]
        passed = pos >= end
        start = jnp.where(passed, end, start)
        doc = doc + passed.astype(jnp.int32)
    in_group = me % GROUP
    base = me - in_group
    for j in range(GROUP + 1):
        if j < GROUP:
            block = base + j - jnp.where(j >= in_group, GROUP, 0)
        else:
            block = me
        key_pos = block * ROWS + lane
        ok = (key_pos >= start) & (key_pos <= pos)
        bias_ref[:, j * 128 : (j + 1) * 128] = jnp.where(ok, 0.0, NEG_BIG)

    keys = kv_ref[:, :HD]
    values = kv_ref[:, HD:]
    own_keys = own_ref[:, :HD]
    own_values = own_ref[:, HD:]
    far = GROUP * ROWS
    best = jnp.full((ROWS, 128), NEG_BIG, jnp.float32)
    n = HEADS_AT_ONCE
    for h0 in range(0, HEADS, n):
        q = q_scr[h0 * ROWS : (h0 + n) * ROWS, :]
        s_far = dot_nt(q, keys).reshape(n, ROWS, far) + bias_ref[:, :far][None]
        s_own = dot_nt(q, own_keys).reshape(n, ROWS, ROWS) + bias_ref[:, far:][None]
        top = jnp.maximum(
            jnp.max(s_far, axis=2, keepdims=True), jnp.max(s_own, axis=2, keepdims=True)
        )
        w_far = jnp.exp2((s_far - top) * SCALE_LOG2E)
        w_own = jnp.exp2((s_own - top) * SCALE_LOG2E)
        total = jnp.sum(w_far, axis=2, keepdims=True) + jnp.sum(w_own, axis=2, keepdims=True)
        acc = jnp.dot(
            w_far.astype(jnp.bfloat16).reshape(n * ROWS, far),
            values,
            preferred_element_type=jnp.float32,
        ) + jnp.dot(
            w_own.astype(jnp.bfloat16).reshape(n * ROWS, ROWS),
            own_values,
            preferred_element_type=jnp.float32,
        )
        context = acc.reshape(n, ROWS, HD) / total
        for k in range(n):
            h = h0 + k
            out_ref[:, h * HD : (h + 1) * HD] = context[k].astype(jnp.bfloat16)
            hit = lane % 64 == h * DOCS + doc
            best = jnp.maximum(best, jnp.where(hit, top[k] * SCALE, NEG_BIG))
    most = jnp.max(best, axis=0, keepdims=True)
    first = most.astype(jnp.bfloat16).astype(jnp.float32)
    second = (most - first).astype(jnp.bfloat16).astype(jnp.float32)
    third = most - first - second
    low = lane < 64
    even = row % 2 == 0
    parts = jnp.where(even, jnp.where(low, first, second), jnp.where(low, third, 0.0))
    out_ref[:, HEADS * HD :] = parts.astype(jnp.bfloat16)


def attend(doc_lengths, source_row, queries, kv_window, kv_own):
    vmem = pl.BlockSpec(memory_space=pltpu.VMEM)
    return pl.pallas_call(
        attend_kernel,
        out_shape=jax.ShapeDtypeStruct((ROWS, HEADS * HD + 128), jnp.bfloat16),
        in_specs=[pl.BlockSpec(memory_space=pltpu.SMEM), vmem, vmem, vmem, vmem],
        out_specs=vmem,
        scratch_shapes=[
            pltpu.VMEM((ROWS, (GROUP + 1) * ROWS), jnp.float32),
            pltpu.VMEM((HEADS * ROWS, HD), jnp.bfloat16),
        ],
        compiler_params=pltpu.CompilerParams(vmem_limit_bytes=40 * 1024 * 1024),
        name="attend",
    )(doc_lengths, source_row, queries, kv_window, kv_own)


def body(queries, keys, values, doc_lengths, source_row):
    me = lax.axis_index("ctx")
    own = jnp.concatenate([keys, values], axis=1)
    before = lax.ppermute(own, "ctx", [(c, c + GROUP) for c in range(CTX - GROUP)])
    groups = [[g * GROUP + i for i in range(GROUP)] for g in range(CTX // GROUP)]
    later = jnp.arange(GROUP, dtype=jnp.int32) > me % GROUP
    slots = jnp.where(later[:, None, None], own[None], before[None])
    window = lax.all_to_all(
        slots, "ctx", split_axis=0, concat_axis=0, tiled=True, axis_index_groups=groups
    ).reshape(GROUP * ROWS, 2 * HD)
    sent = attend(doc_lengths, source_row, queries, window, own)
    got = lax.all_to_all(
        sent.reshape(CTX, 2, HEADS * HD + 128), "ctx", split_axis=0, concat_axis=0, tiled=True
    )
    context = got[:, :, : HEADS * HD].reshape(ROWS, HEADS * HD)
    parts = got[:, :, HEADS * HD :].astype(jnp.float32)
    maxima = jnp.max(parts[:, 0, :64] + (parts[:, 0, 64:] + parts[:, 1, :64]), axis=0)
    all_maxima = lax.all_gather(maxima.reshape(HEADS, DOCS), "head", axis=0, tiled=True)
    return (context, all_maxima)


def solution(mesh):
    return jax.shard_map(
        body,
        mesh=mesh,
        in_specs=(P("ctx", "head"), P("ctx", "head"), P("ctx", "head"), P(), P()),
        out_specs=(P("ctx", "head"), P()),
        check_vma=False,
    )
```

time: 539 us -> 83.6 us (0.16)
  waiting for transfers between devices: 204 us -> 1.29 us
  blocking collectives: 230 us -> 67 us
  matrix products: 47.9 us -> 0 us
  local copies, waits for them, and re-layouts: 20.6 us -> 3.28 us
  other arithmetic: 14.8 us -> 0.32 us
  between operations: 14.2 us -> 0.73 us
    all_gather x2 -> x0, waiting for transfers between devices: 193 us -> none  [the longest x1 119 us: gather_for_moved(): lax.all_gather(value_rows, 'ctx', axis=0, tiled=True)]
    pmax x1 -> x0, blocking collectives: 152 us -> none  [body(): reduced = lax.pmax(local_max, 'ctx')]
    dot_general x32 -> x0, matrix products: 47.9 us -> none  [the longest x16 26 us: block_update(): jnp.einsum('tkgj,jkd->tkgd', weights.astype(jnp.bfloat16), value_heads, p...]
    all_gather x1, blocking collectives: 36.8 us -> 8.82 us  [body(): lax.all_gather(maxima.reshape(HEADS, DOCS), 'head', axis=0, tiled=True)]
    all_to_all x2, blocking collectives: 41.2 us -> 58.2 us  [the longest x1 32.9 us: body(): lax.all_to_all(slots, 'ctx', split_axis=0, concat_axis=0, tiled=True, axi...]
    dynamic_slice x18 -> x0, local copies, waits for them, and re-layouts: 13.8 us -> none  [the longest x16 12.2 us: one_block(): lax.dynamic_slice_in_dim(piece_pos, offset, block_len, 0)]
    all_to_all x1 -> x0, waiting for transfers between devices: 10.8 us -> none  [body(): lax.all_to_all(outgoing(queries), 'ctx', split_axis=0, concat_axis=0, til...]
    reduce_sum x33 -> x0, other arithmetic: 9.71 us -> none  [the longest x16 8.24 us: block_update(): row_total = row_total * factor + jnp.sum(weights, axis=3)]
  transfers between devices with their start and end apart: 3 -> 1, of which waited for: 3 -> 1; matrix products, arithmetic and copies ran while one was open for 1% -> 0% of each run, Pallas kernels for 0% -> 0%
where the time goes in v1:
time: 83.6 us; the launch traced here: 83.3 us
  blocking collectives  67 us (80%)
  starting transfers between devices  5.65 us (7%)
  Pallas kernels  5 us (6%)
  local copies, waits for them, and re-layouts  3.28 us (4%)
  waiting for transfers between devices  1.29 us (2%)
    all_to_all x1, blocking collectives, body(): lax.all_to_all(slots, 'ctx', split_axis=0, concat_axis=0, tiled=True, axi...  32.9 us
    all_to_all x1, blocking collectives, body(): lax.all_to_all(sent.reshape(CTX, 2, HEADS * HD + 128), 'ctx', split_axis=...  25.4 us
    all_gather x1, blocking collectives, body(): lax.all_gather(maxima.reshape(HEADS, DOCS), 'head', axis=0, tiled=True)  8.82 us
    ppermute x1, starting transfers between devices, body(): lax.ppermute(own, 'ctx', [(c, c + GROUP) for c in range(CTX - GROUP)])  5.65 us
    pallas_call x1, Pallas kernels, attend(): pl.pallas_call(attend_kernel, out_shape=jax.ShapeDtypeStruct((ROWS, HEADS...  5 us
    unnamed x10, local copies, waits for them, and re-layouts  2.1 us
  transfers between devices with their start and end apart: 1, of which 1 were waited for; matrix products, arithmetic and copies ran while one was open for 0% of the time, Pallas kernels for 0%

profile of v1, /device:TPU:1, one launch (start us, length us, event | category | flops | bytes accessed | tf_op | source)
XLA Modules:
  0.0 83.3 jit_solution(14966988685710026427)
XLA Ops:
  0.6 0.0 copy-start.3
  0.6 0.8 constant_dynamic-update-slice_fusion.1
  1.4 0.0 copy-done.3
  1.4 5.7 %collective-permute-start = (bf16[128,256]{1,0:T(8,128)(2,1)S(1)}, bf16[128,256]{1,0:T(8,128)(2,1)S(1)}, u32[]{:S(2)}, u32[]{:S(2)}) collective-permute-start(bf16[128,256]{1,0:T(8,128)(2,1)S(1)} %constant_dynamic-update-slice_fusion.own_ref), channel_id=1, source_target_pairs={{0,64},{4,68},{8,72},{12,76},{16,80},{20,84},{24,88},{28,92},{32,9... | collective-permute-start | bytes 196616 | tf_op jit(solution)/shard_map/ppermute | solution.py:126
  7.1 1.3 %collective-permute-done = bf16[128,256]{1,0:T(8,128)(2,1)S(1)} collective-permute-done((bf16[128,256]{1,0:T(8,128)(2,1)S(1)}, bf16[128,256]{1,0:T(8,128)(2,1)S(1)}, u32[]{:S(2)}, u32[]{:S(2)}) %collective-permute-start) | collective-permute-done | bytes 65568 | tf_op jit(solution)/shard_map/ppermute | solution.py:126
  8.4 0.1 broadcast_select_fusion
  8.5 0.0 copy-start
  8.6 0.0 copy-start.1
  8.6 32.9 %all_to_all.10 = bf16[16,128,256]{2,1,0:T(8,128)(2,1)S(1)} all-to-all(bf16[16,128,256]{2,1,0:T(8,128)(2,1)S(1)} %broadcast_select_fusion), channel_id=1, replica_groups={{0,4,8,12,16,20,24,28,32,36,40,44,48,52,56,60},{64,68,72,76,80,84,88,92..., dimensions={0} | all-to-all | bytes 2097152 | tf_op jit(solution)/shard_map/all_to_all | solution.py:130
  41.4 0.0 copy-start.2
  41.4 0.0 copy-done
  41.4 0.0 copy-done.1
  41.4 0.6 copy-done.2
  42.1 5.0 %attend.1 = bf16[128,1152]{1,0:T(8,128)(2,1)S(1)} custom-call(s32[8]{0:T(128)S(1)} %copy-done.2, s32[64,128]{1,0:T(8,128)S(1)} %copy-done.1, bf16[128,1024]{1,0:T(8,128)(2,1)S(1)} %copy-done, bf16[2048,256]{1,0:T(8,128)(2,1)S(1)} %bitcast.1, bf16[128,256]{1,0:T(8,128)(2,1)S(1)} %constant_dynamic-update-slice_fusion.own_ref), custom_call_target="tpu_custom_call" | custom-call | tf_op jit(solution)/shard_map/attend/pallas_call | solution.py:109
  47.1 0.1 reshape.25
  47.2 25.4 %all_to_all.11 = bf16[64,2,1152]{2,1,0:T(2,128)(2,1)S(1)} all-to-all(bf16[64,2,1152]{2,1,0:T(2,128)(2,1)S(1)} %reshape.25), channel_id=1, replica_groups=mesh['ctx'=64,'head'=4] {'ctx'}, dimensions={0} | all-to-all | bytes 589824 | tf_op jit(solution)/shard_map/all_to_all | solution.py:134
  72.6 0.2 fusion.1
  72.8 0.2 slice.20
  72.9 0.8 reshape.26
  73.7 0.1 reshape.27
  73.8 8.8 %all_gather.3 = f32[32,8]{1,0:T(8,128)S(1)} all-gather(f32[8,8]{1,0:T(8,128)S(1)} %reshape.27), channel_id=1, replica_groups=mesh['ctx'=64,'head'=4] {'head'}, dimensions={0}, use_global_device_ids=true | all-gather | bytes 1280 | tf_op jit(solution)/shard_map/all_gather | solution.py:140
  82.6 0.7 copy.7
  (3 shorter events, 0.0 us)
Async XLA Ops:
  0.6 0.8 copy-start.3
  1.4 7.0 %collective-permute-start = (bf16[128,256]{1,0:T(8,128)(2,1)S(1)}, bf16[128,256]{1,0:T(8,128)(2,1)S(1)}, u32[]{:S(2)}, u32[]{:S(2)}) collective-permute-start(bf16[128,256]{1,0:T(8,128)(2,1)S(1)} %constant_dynamic-update-slice_fusion.own_ref), channel_id=1, source_target_pairs={{0,64},{4,68},{8,72},{12,76},{16,80},{20,84},{24,88},{28,92},{32,9... | collective-permute-start | bytes 196616 | tf_op jit(solution)/shard_map/ppermute | solution.py:126
  8.5 32.9 %copy-start = (bf16[128,1024]{1,0:T(8,128)(2,1)S(1)}, bf16[128,1024]{1,0:T(8,128)(2,1)}, u32[]{:S(2)}) copy-start(bf16[128,1024]{1,0:T(8,128)(2,1)} %q_ref.1) | copy-start | bytes 786436
  8.6 32.9 %copy-start.1 = (s32[64,128]{1,0:T(8,128)S(1)}, s32[64,128]{1,0:T(8,128)}, u32[]{:S(2)}) copy-start(s32[64,128]{1,0:T(8,128)} %source_ref.1) | copy-start | bytes 98308
  41.4 0.7 copy-start.2

commit v2 on v1

v2 whole, which is shorter than its diff:
```python
import math

import jax
import jax.numpy as jnp
from jax import lax
from jax.experimental import pallas as pl
from jax.experimental.pallas import tpu as pltpu
from jax.sharding import PartitionSpec as P

HD = 128
HEADS = 8
DOCS = 8
ROWS = 128
RING = 8
CTX = 64
WIDE = HEADS * HD
PART = WIDE + 128
NEG_BIG = -1e30
SCALE = 1.0 / math.sqrt(HD)
SCALE_LOG2E = SCALE * math.log2(math.e)
HEADS_AT_ONCE = 2
FAR = RING * ROWS


def dot_nt(a, b):
    return lax.dot_general(a, b, (((1,), (1,)), ((), ())), preferred_element_type=jnp.float32)


def as_bf16(mask):
    return mask.astype(jnp.float32).astype(jnp.bfloat16)


def three_parts(x):
    first = x.astype(jnp.bfloat16).astype(jnp.float32)
    second = (x - first).astype(jnp.bfloat16).astype(jnp.float32)
    return first, second, x - first - second


def iota(shape, dim):
    return lax.broadcasted_iota(jnp.int32, shape, dim)


def attend_kernel(
    lengths_ref, source_ref, q_ref, next_q_ref, kv_ref, own_ref, out_ref, bias_ref, q_scr
):
    me = lax.axis_index("ctx")
    lane = iota((ROWS, 128), 1)
    row = iota((ROWS, 128), 0)
    local = as_bf16(source_ref[...] - iota((CTX, 128), 1) // 2 * ROWS)
    spread = as_bf16(iota((ROWS, CTX), 0) // 2 == iota((ROWS, CTX), 1))
    table = jnp.dot(spread, local, preferred_element_type=jnp.float32)
    in_ring = me % RING
    base = me - in_ring
    best = jnp.full((ROWS, 128), NEG_BIG, jnp.float32)
    logs = []
    n = HEADS_AT_ONCE
    for part, rows_ref in ((0, q_ref), (1, next_q_ref)):
        chunk = me + RING * part
        pick = jnp.sum(
            jnp.where(lane == 2 * chunk + row % 2, table, 0.0), axis=1, keepdims=True
        ).astype(jnp.int32)
        q_all = jnp.dot(as_bf16(lane == pick), rows_ref[...], preferred_element_type=jnp.float32)
        for h in range(HEADS):
            q_scr[h * ROWS : (h + 1) * ROWS, :] = q_all[:, h * HD : (h + 1) * HD].astype(
                jnp.bfloat16
            )
        pos = chunk * ROWS + pick
        start = jnp.zeros_like(pos)
        doc = jnp.zeros_like(pos)
        end = jnp.int32(0)
        for i in range(DOCS):
            end = end + lengths_ref[i]
            passed = pos >= end
            start = jnp.where(passed, end, start)
            doc = doc + passed.astype(jnp.int32)
        for j in range(RING + 1):
            if j < RING:
                block = base + j - jnp.where(j >= in_ring, RING, 0)
            else:
                block = me
            key_pos = block * ROWS + lane
            ok = (key_pos >= start) & (key_pos <= pos)
            if part == 0:
                ok = ok & (block > me - RING)
            bias_ref[:, j * 128 : (j + 1) * 128] = jnp.where(ok, 0.0, NEG_BIG)

        log_total = jnp.zeros((ROWS, 128), jnp.float32)
        for h0 in range(0, HEADS, n):
            q = q_scr[h0 * ROWS : (h0 + n) * ROWS, :]
            s_far = dot_nt(q, kv_ref[:, :HD]).reshape(n, ROWS, FAR) + bias_ref[:, :FAR][None]
            s_own = dot_nt(q, own_ref[:, :HD]).reshape(n, ROWS, ROWS) + bias_ref[:, FAR:][None]
            top = jnp.maximum(
                jnp.max(s_far, axis=2, keepdims=True), jnp.max(s_own, axis=2, keepdims=True)
            )
            w_far = jnp.exp2((s_far - top) * SCALE_LOG2E)
            w_own = jnp.exp2((s_own - top) * SCALE_LOG2E)
            total = jnp.sum(w_far, axis=2, keepdims=True) + jnp.sum(w_own, axis=2, keepdims=True)
            acc = jnp.dot(
                w_far.astype(jnp.bfloat16).reshape(n * ROWS, FAR),
                kv_ref[:, HD:],
                preferred_element_type=jnp.float32,
            ) + jnp.dot(
                w_own.astype(jnp.bfloat16).reshape(n * ROWS, ROWS),
                own_ref[:, HD:],
                preferred_element_type=jnp.float32,
            )
            context = acc.reshape(n, ROWS, HD) / total
            for k in range(n):
                h = h0 + k
                at = part * PART + h * HD
                out_ref[:, at : at + HD] = context[k].astype(jnp.bfloat16)
                peak = top[k] * SCALE
                best = jnp.maximum(
                    best, jnp.where(lane == h * DOCS + doc, peak, NEG_BIG)
                )
                log_total = jnp.where(lane % 8 == h, peak + jnp.log(total[k]), log_total)
        logs.append(log_total)

    most = three_parts(jnp.max(best, axis=0, keepdims=True))
    even = row % 2 == 0
    for part in range(2):
        first, second, third = three_parts(logs[part])
        tail = jnp.where(lane < 72, first, jnp.where(lane < 80, second, third))
        if part == 0:
            head = jnp.where(even, most[0], most[1])
        else:
            head = jnp.where(even, most[2], 0.0)
        at = part * PART + WIDE
        out_ref[:, at : at + 128] = jnp.where(lane < 64, head, tail).astype(jnp.bfloat16)


def merge_kernel(got_ref, out_ref, maxima_ref):
    lane = iota((ROWS, 128), 1)
    row = iota((ROWS, 128), 0)
    shift = 2 * RING
    near = got_ref[:, WIDE : WIDE + 128].astype(jnp.float32)
    far = got_ref[:, PART + WIDE : PART + WIDE + 128].astype(jnp.float32)

    most = near + (pltpu.roll(near, ROWS - 1, 0) + far)
    most = jnp.max(jnp.where(row % 2 == 0, most, NEG_BIG), axis=0, keepdims=True)
    lane8 = iota((HEADS, 128), 1)
    spread = jnp.where(lane8 // DOCS == iota((HEADS, 128), 0), most, 0.0)
    fold = as_bf16(
        (iota((128, DOCS), 0) % DOCS == iota((128, DOCS), 1)) & (iota((128, DOCS), 0) < 64)
    )
    folded = [
        jnp.dot(p.astype(jnp.bfloat16), fold, preferred_element_type=jnp.float32)
        for p in three_parts(spread)
    ]
    maxima_ref[...] = folded[0] + (folded[1] + folded[2])

    def whole(x):
        return x + (pltpu.roll(x, 128 - 8, 1) + pltpu.roll(x, 128 - 16, 1))

    log_near = whole(near)
    log_far = pltpu.roll(whole(far), shift, 0)
    weight = 1.0 / (1.0 + jnp.exp(log_far - log_near))
    weight = jnp.where(row < shift, 1.0, weight)
    for h in range(HEADS):
        w = weight[:, 64 + h : 65 + h]
        mine = got_ref[:, h * HD : (h + 1) * HD].astype(jnp.float32)
        other = got_ref[:, PART + h * HD : PART + (h + 1) * HD].astype(jnp.float32)
        other = pltpu.roll(other, shift, 0)
        out_ref[:, h * HD : (h + 1) * HD] = (mine * w + other * (1.0 - w)).astype(jnp.bfloat16)


VMEM = pl.BlockSpec(memory_space=pltpu.VMEM)
SMEM = pl.BlockSpec(memory_space=pltpu.SMEM)


def attend(doc_lengths, source_row, queries, next_queries, window, own):
    return pl.pallas_call(
        attend_kernel,
        out_shape=jax.ShapeDtypeStruct((ROWS, 2 * PART), jnp.bfloat16),
        in_specs=[SMEM, VMEM, VMEM, VMEM, VMEM, VMEM],
        out_specs=VMEM,
        scratch_shapes=[
            pltpu.VMEM((ROWS, FAR + ROWS), jnp.float32),
            pltpu.VMEM((HEADS * ROWS, HD), jnp.bfloat16),
        ],
        compiler_params=pltpu.CompilerParams(vmem_limit_bytes=40 * 1024 * 1024),
        name="attend",
    )(doc_lengths, source_row, queries, next_queries, window, own)


def merge(got):
    return pl.pallas_call(
        merge_kernel,
        out_shape=(
            jax.ShapeDtypeStruct((ROWS, WIDE), jnp.bfloat16),
            jax.ShapeDtypeStruct((HEADS, DOCS), jnp.float32),
        ),
        in_specs=[VMEM],
        out_specs=(VMEM, VMEM),
        compiler_params=pltpu.CompilerParams(vmem_limit_bytes=40 * 1024 * 1024),
        name="merge",
    )(got)


def body(queries, keys, values, doc_lengths, source_row):
    me = lax.axis_index("ctx")
    own = jnp.concatenate([keys, values], axis=1)
    before = lax.ppermute(own, "ctx", [(c, c + RING) for c in range(CTX - RING)])
    next_queries = lax.ppermute(queries, "ctx", [(c + RING, c) for c in range(CTX - RING)])
    rings = [[r * RING + i for i in range(RING)] for r in range(CTX // RING)]
    later = jnp.arange(RING, dtype=jnp.int32) > me % RING
    slots = jnp.where(later[:, None, None], own[None], before[None])
    window = lax.all_to_all(
        slots, "ctx", split_axis=0, concat_axis=0, tiled=True, axis_index_groups=rings
    ).reshape(FAR, 2 * HD)
    sent = attend(doc_lengths, source_row, queries, next_queries, window, own)
    got = lax.all_to_all(
        sent.reshape(CTX, 2, 2 * PART), "ctx", split_axis=0, concat_axis=0, tiled=True
    )
    context, maxima = merge(got.reshape(ROWS, 2 * PART))
    all_maxima = lax.all_gather(maxima, "head", axis=0, tiled=True)
    return (context, all_maxima)


def solution(mesh):
    return jax.shard_map(
        body,
        mesh=mesh,
        in_specs=(P("ctx", "head"), P("ctx", "head"), P("ctx", "head"), P(), P()),
        out_specs=(P("ctx", "head"), P()),
        check_vma=False,
    )
```

time: 83.6 us -> 77 us (0.921)
  blocking collectives: 67 us -> 36.6 us
  waiting for transfers between devices: 1.29 us -> 15.9 us
  starting transfers between devices: 5.65 us -> 13.6 us
  Pallas kernels: 5 us -> 6.97 us
  local copies, waits for them, and re-layouts: 3.28 us -> 1.91 us
    all_to_all x2 -> x1, blocking collectives: 58.2 us -> 26.7 us  [body(): lax.all_to_all(sent.reshape(CTX, 2, 2 * PART), 'ctx', split_axis=0, conca...]
    all_to_all x0 -> x1, starting transfers between devices: none -> 8.32 us  [body(): lax.all_to_all(slots, 'ctx', split_axis=0, concat_axis=0, tiled=True, axi...]
    all_to_all x0 -> x1, waiting for transfers between devices: none -> 7.72 us  [body(): lax.all_to_all(slots, 'ctx', split_axis=0, concat_axis=0, tiled=True, axi...]
    ppermute x1 -> x2, waiting for transfers between devices: 1.29 us -> 8.18 us  [the longest x1 6.9 us: body(): lax.ppermute(queries, 'ctx', [(c + RING, c) for c in range(CTX - RING)])]
    pallas_call x1 -> x2, Pallas kernels: 5 us -> 6.97 us  [the longest x1 5.82 us: attend(): pl.pallas_call(attend_kernel, out_shape=jax.ShapeDtypeStruct((ROWS, 2 * P...]
    all_gather x1, blocking collectives: 8.82 us -> 9.95 us  [body(): all_maxima = lax.all_gather(maxima, 'head', axis=0, tiled=True)]
    ppermute x1 -> x2, starting transfers between devices: 5.65 us -> 5.33 us  [the longest x1 4.03 us: body(): lax.ppermute(own, 'ctx', [(c, c + RING) for c in range(CTX - RING)])]
  transfers between devices with their start and end apart: 1 -> 3, of which waited for: 1 -> 3; matrix products, arithmetic and copies ran while one was open for 0% -> 0% of each run, Pallas kernels for 0% -> 0%
where the time goes in v2:
time: 77 us; the launch traced here: 76.7 us
  blocking collectives  36.6 us (48%)
  waiting for transfers between devices  15.9 us (21%)
  starting transfers between devices  13.6 us (18%)
  Pallas kernels  6.97 us (9%)
  local copies, waits for them, and re-layouts  1.91 us (2%)
  other arithmetic  0.91 us (1%)
    all_to_all x1, blocking collectives, body(): lax.all_to_all(sent.reshape(CTX, 2, 2 * PART), 'ctx', split_axis=0, conca...  26.7 us
    all_gather x1, blocking collectives, body(): all_maxima = lax.all_gather(maxima, 'head', axis=0, tiled=True)  9.95 us
    all_to_all x1, starting transfers between devices, body(): lax.all_to_all(slots, 'ctx', split_axis=0, concat_axis=0, tiled=True, axi...  8.32 us
    all_to_all x1, waiting for transfers between devices, body(): lax.all_to_all(slots, 'ctx', split_axis=0, concat_axis=0, tiled=True, axi...  7.72 us
    ppermute x1, waiting for transfers between devices, body(): lax.ppermute(queries, 'ctx', [(c + RING, c) for c in range(CTX - RING)])  6.9 us
    pallas_call x1, Pallas kernels, attend(): pl.pallas_call(attend_kernel, out_shape=jax.ShapeDtypeStruct((ROWS, 2 * P...  5.82 us
    ppermute x1, starting transfers between devices, body(): lax.ppermute(own, 'ctx', [(c, c + RING) for c in range(CTX - RING)])  4.03 us
  transfers between devices with their start and end apart: 3, of which 3 were waited for; matrix products, arithmetic and copies ran while one was open for 0% of the time, Pallas kernels for 0%

profile of v2, /device:TPU:1, one launch (start us, length us, event | category | flops | bytes accessed | tf_op | source)
XLA Modules:
  0.0 76.7 jit_solution(17546612709806195050)
XLA Ops:
  0.6 0.0 copy-start.3
  0.6 0.8 %constant_dynamic-update-slice_fusion.1 = bf16[128,256]{1,0:T(8,128)(2,1)S(1)} fusion(bf16[128,128]{1,0:T(8,128)(2,1)} %param.6), kind=kLoop, calls=%fused_computation.2 | loop fusion | bytes 65536
  1.4 0.0 copy-done.3
  1.4 4.0 %collective-permute-start.1 = (bf16[128,256]{1,0:T(8,128)(2,1)S(1)}, bf16[128,256]{1,0:T(8,128)(2,1)S(1)}, u32[]{:S(2)}, u32[]{:S(2)}) collective-permute-start(bf16[128,256]{1,0:T(8,128)(2,1)S(1)} %constant_dynamic-update-slice_fusion.own_ref), channel_id=1, source_target_pairs={{0,32},{4,36},{8,40},{12,44},{16,48},{20,52},{24,56},{28,60},{32,6... | collective-permute-start | bytes 196616 | tf_op jit(solution)/shard_map/ppermute | solution.py:203
  5.5 1.3 %collective-permute-done.1 = bf16[128,256]{1,0:T(8,128)(2,1)S(1)} collective-permute-done((bf16[128,256]{1,0:T(8,128)(2,1)S(1)}, bf16[128,256]{1,0:T(8,128)(2,1)S(1)}, u32[]{:S(2)}, u32[]{:S(2)}) %collective-permute-start.1) | collective-permute-done | bytes 65568 | tf_op jit(solution)/shard_map/ppermute | solution.py:203
  6.8 0.9 %broadcast_select_fusion = bf16[8,128,256]{2,1,0:T(8,128)(2,1)} fusion(pred[8]{0:T(512)(128)(4,1)S(1)} %iota_compare_fusion, bf16[128,256]{1,0:T(8,128)(2,1)S(1)} %collective-permute-done.1, bf16[128,256]{1,0:T(8,128)(2,1)S(1)} %constant_dynamic-update-slice_fusion.own_ref), kind=kLoop, calls=%fused_computation | loop fusion | flops 262144 | bytes 655368 | tf_op jit(solution)/shard_map/jit(_where)/select_n | solution.py:207
  7.7 0.0 copy-start
  7.7 0.0 copy-start.1
  7.7 8.3 %all-to-all-start = ((bf16[8,128,256]{2,1,0:T(8,128)(2,1)}), bf16[8,128,256]{2,1,0:T(8,128)(2,1)S(1)}, u32[]{:S(2)}, u32[]{:S(2)}) async-start(bf16[8,128,256]{2,1,0:T(8,128)(2,1)} %broadcast_select_fusion), calls=%async_computation | async-start | bytes 1048576 | tf_op jit(solution)/shard_map/all_to_all | solution.py:208
  16.0 0.0 copy-done
  16.0 0.0 copy-start.2
  16.0 1.3 %collective-permute-start = (bf16[128,1024]{1,0:T(8,128)(2,1)S(1)}, bf16[128,1024]{1,0:T(8,128)(2,1)S(1)}, u32[]{:S(2)}, u32[]{:S(2)}) collective-permute-start(bf16[128,1024]{1,0:T(8,128)(2,1)S(1)} %copy-done), channel_id=1, source_target_pairs={{32,0},{36,4},{40,8},{44,12},{48,16},{52,20},{56,24},{60,28},{64,3... | collective-permute-start | bytes 786440 | tf_op jit(solution)/shard_map/ppermute | solution.py:204
  17.3 6.9 %collective-permute-done.next_q_ref = bf16[128,1024]{1,0:T(8,128)(2,1)S(1)} collective-permute-done((bf16[128,1024]{1,0:T(8,128)(2,1)S(1)}, bf16[128,1024]{1,0:T(8,128)(2,1)S(1)}, u32[]{:S(2)}, u32[]{:S(2)}) %collective-permute-start) | collective-permute-done | bytes 262176 | tf_op jit(solution)/shard_map/ppermute | solution.py:204
  24.2 7.7 %all-to-all-done = bf16[8,128,256]{2,1,0:T(8,128)(2,1)S(1)} async-done(((bf16[8,128,256]{2,1,0:T(8,128)(2,1)}), bf16[8,128,256]{2,1,0:T(8,128)(2,1)S(1)}, u32[]{:S(2)}, u32[]{:S(2)}) %all-to-all-start) | async-done | bytes 524320 | tf_op jit(solution)/shard_map/all_to_all | solution.py:208
  32.0 0.0 copy-done.1
  32.0 0.0 copy-done.2
  32.0 5.8 %attend.1 = bf16[128,2304]{1,0:T(8,128)(2,1)S(1)} custom-call(s32[8]{0:T(128)S(1)} %copy-done.2, s32[64,128]{1,0:T(8,128)S(1)} %copy-done.1, bf16[128,1024]{1,0:T(8,128)(2,1)S(1)} %copy-done, bf16[128,1024]{1,0:T(8,128)(2,1)S(1)} %collective-permute-done.next_q_ref, bf16[1024,256]{1,0:T(8,128)(2,1)S(1)} %bitcast.1, ...), custom_call_target="tpu_custom_call" | custom-call | tf_op jit(solution)/shard_map/attend/pallas_call | solution.py:172
  37.8 0.2 reshape.20
  38.0 26.7 %all_to_all.10 = bf16[64,2,2304]{2,1,0:T(2,128)(2,1)S(1)} all-to-all(bf16[64,2,2304]{2,1,0:T(2,128)(2,1)S(1)} %reshape.20), channel_id=1, replica_groups=mesh['ctx'=64,'head'=4] {'ctx'}, dimensions={0} | all-to-all | bytes 1179648 | tf_op jit(solution)/shard_map/all_to_all | solution.py:212
  64.7 0.2 reshape.21.got_ref
  64.9 1.2 %merge.1 = (bf16[128,1024]{1,0:T(8,128)(2,1)}, f32[8,8]{1,0:T(8,128)S(1)}) custom-call(bf16[128,2304]{1,0:T(8,128)(2,1)S(1)} %reshape.21.got_ref), custom_call_target="tpu_custom_call" | custom-call | tf_op jit(solution)/shard_map/merge/pallas_call | solution.py:187
  66.1 9.9 %all_gather.3 = f32[32,8]{1,0:T(8,128)S(1)} all-gather(f32[8,8]{1,0:T(8,128)S(1)} %get-tuple-element.5), channel_id=1, replica_groups=mesh['ctx'=64,'head'=4] {'head'}, dimensions={0}, use_global_device_ids=true | all-gather | bytes 1280 | tf_op jit(solution)/shard_map/all_gather | solution.py:216
  76.0 0.7 copy.7
  (2 shorter events, 0.0 us)
Async XLA Ops:
  0.6 0.8 %copy-start.3 = (bf16[128,128]{1,0:T(8,128)(2,1)S(1)}, bf16[128,128]{1,0:T(8,128)(2,1)}, u32[]{:S(2)}) copy-start(bf16[128,128]{1,0:T(8,128)(2,1)} %param.7) | copy-start | bytes 98308
  1.4 5.4 %collective-permute-start.1 = (bf16[128,256]{1,0:T(8,128)(2,1)S(1)}, bf16[128,256]{1,0:T(8,128)(2,1)S(1)}, u32[]{:S(2)}, u32[]{:S(2)}) collective-permute-start(bf16[128,256]{1,0:T(8,128)(2,1)S(1)} %constant_dynamic-update-slice_fusion.own_ref), channel_id=1, source_target_pairs={{0,32},{4,36},{8,40},{12,44},{16,48},{20,52},{24,56},{28,60},{32,6... | collective-permute-start | bytes 196616 | tf_op jit(solution)/shard_map/ppermute | solution.py:203
  7.7 8.3 %copy-start = (bf16[128,1024]{1,0:T(8,128)(2,1)S(1)}, bf16[128,1024]{1,0:T(8,128)(2,1)}, u32[]{:S(2)}) copy-start(bf16[128,1024]{1,0:T(8,128)(2,1)} %q_ref.1) | copy-start | bytes 786436
  7.7 24.3 %copy-start.1 = (s32[64,128]{1,0:T(8,128)S(1)}, s32[64,128]{1,0:T(8,128)}, u32[]{:S(2)}) copy-start(s32[64,128]{1,0:T(8,128)} %source_ref.1) | copy-start | bytes 98308
  7.7 24.3 %all-to-all-start = ((bf16[8,128,256]{2,1,0:T(8,128)(2,1)}), bf16[8,128,256]{2,1,0:T(8,128)(2,1)S(1)}, u32[]{:S(2)}, u32[]{:S(2)}) async-start(bf16[8,128,256]{2,1,0:T(8,128)(2,1)} %broadcast_select_fusion), calls=%async_computation | async-start | bytes 1048576 | tf_op jit(solution)/shard_map/all_to_all | solution.py:208
  16.0 15.9 %copy-start.2 = (s32[8]{0:T(128)S(1)}, s32[8]{0:T(128)}, u32[]{:S(2)}) copy-start(s32[8]{0:T(128)} %lengths_ref.1) | copy-start | bytes 100
  16.0 8.2 %collective-permute-start = (bf16[128,1024]{1,0:T(8,128)(2,1)S(1)}, bf16[128,1024]{1,0:T(8,128)(2,1)S(1)}, u32[]{:S(2)}, u32[]{:S(2)}) collective-permute-start(bf16[128,1024]{1,0:T(8,128)(2,1)S(1)} %copy-done), channel_id=1, source_target_pairs={{32,0},{36,4},{40,8},{44,12},{48,16},{52,20},{56,24},{60,28},{64,3... | collective-permute-start | bytes 786440 | tf_op jit(solution)/shard_map/ppermute | solution.py:204

commit v3 on v2

v3 whole, which is shorter than its diff:
```python
import math

import jax
import jax.numpy as jnp
from jax import lax
from jax.experimental import pallas as pl
from jax.experimental.pallas import tpu as pltpu
from jax.sharding import PartitionSpec as P

HD = 128
HEADS = 8
GROUPS = 4
DOCS = 8
ROWS = 128
RING = 8
RINGS = 8
CTX = RING * RINGS
PARTS = 2
WIDE = HEADS * HD
FAR = RING * ROWS
WINDOW = FAR + ROWS
NEG_BIG = -1e30
SCALE = 1.0 / math.sqrt(HD)
SCALE_LOG2E = SCALE * math.log2(math.e)
HEADS_AT_ONCE = 4
SPAN = GROUPS * HEADS


def dot_nt(a, b):
    return lax.dot_general(a, b, (((1,), (1,)), ((), ())), preferred_element_type=jnp.float32)


def as_bf16(mask):
    return mask.astype(jnp.float32).astype(jnp.bfloat16)


def three_parts(x):
    first = x.astype(jnp.bfloat16).astype(jnp.float32)
    second = (x - first).astype(jnp.bfloat16).astype(jnp.float32)
    return first, second, x - first - second


def iota(shape, dim):
    return lax.broadcasted_iota(jnp.int32, shape, dim)


def prepare_kernel(
    lengths_ref, source_ref, q0_ref, q1_ref, q_out, bias_out, doc_out
):
    me = lax.axis_index("ctx")
    lane = iota((ROWS, 128), 1)
    row = iota((ROWS, 128), 0)
    local = as_bf16(source_ref[...] - iota((CTX, 128), 1) // 2 * ROWS)
    spread = as_bf16(iota((ROWS, CTX), 0) // 2 == iota((ROWS, CTX), 1))
    table = jnp.dot(spread, local, preferred_element_type=jnp.float32)
    in_ring = me % RING
    base = me - in_ring
    for part, rows_ref in enumerate((q0_ref, q1_ref)):
        chunk = me + RING * part
        pick = jnp.sum(
            jnp.where(lane == 2 * chunk + row % 2, table, 0.0), axis=1, keepdims=True
        ).astype(jnp.int32)
        q_all = jnp.dot(as_bf16(lane == pick), rows_ref[...], preferred_element_type=jnp.float32)
        for h in range(HEADS):
            q_out[part, h * ROWS : (h + 1) * ROWS, :] = q_all[:, h * HD : (h + 1) * HD].astype(
                jnp.bfloat16
            )
        pos = chunk * ROWS + pick
        start = jnp.zeros_like(pos)
        doc = jnp.zeros_like(pos)
        end = jnp.int32(0)
        for i in range(DOCS):
            end = end + lengths_ref[i]
            passed = pos >= end
            start = jnp.where(passed, end, start)
            doc = doc + passed.astype(jnp.int32)
        doc_out[part] = jnp.broadcast_to(doc, (ROWS, 128))
        for j in range(RING + 1):
            block = me if j == RING else base + j - jnp.where(j >= in_ring, RING, 0)
            key_pos = block * ROWS + lane
            ok = (key_pos >= start) & (key_pos <= pos)
            if part == 0:
                ok = ok & (block > me - RING)
            bias_out[part, :, j * 128 : (j + 1) * 128] = jnp.where(ok, 0.0, NEG_BIG)


def attend_kernel(q_ref, bias_ref, doc_ref, kv_ref, own_ref, out_ref):
    lane = iota((ROWS, 128), 1)
    n = HEADS_AT_ONCE
    all_logs = []
    best = jnp.full((ROWS, 128), NEG_BIG, jnp.float32)
    for part in range(PARTS):
        peaks = jnp.full((ROWS, 128), NEG_BIG, jnp.float32)
        logs = jnp.full((ROWS, 128), NEG_BIG, jnp.float32)
        for h0 in range(0, HEADS, n):
            q = q_ref[part, h0 * ROWS : (h0 + n) * ROWS, :]
            s_far = dot_nt(q, kv_ref[:, :HD]).reshape(n, ROWS, FAR) + bias_ref[part, :, :FAR][None]
            s_own = (
                dot_nt(q, own_ref[:, :HD]).reshape(n, ROWS, ROWS) + bias_ref[part, :, FAR:][None]
            )
            top = jnp.maximum(
                jnp.max(s_far, axis=2, keepdims=True), jnp.max(s_own, axis=2, keepdims=True)
            )
            w_far = jnp.exp2((s_far - top) * SCALE_LOG2E)
            w_own = jnp.exp2((s_own - top) * SCALE_LOG2E)
            total = jnp.sum(w_far, axis=2, keepdims=True) + jnp.sum(w_own, axis=2, keepdims=True)
            acc = jnp.dot(
                w_far.astype(jnp.bfloat16).reshape(n * ROWS, FAR),
                kv_ref[:, HD:],
                preferred_element_type=jnp.float32,
            ) + jnp.dot(
                w_own.astype(jnp.bfloat16).reshape(n * ROWS, ROWS),
                own_ref[:, HD:],
                preferred_element_type=jnp.float32,
            )
            context = acc.reshape(n, ROWS, HD) / total
            for k in range(n):
                h = h0 + k
                at = part * WIDE + h * HD
                out_ref[:, at : at + HD] = context[k].astype(jnp.bfloat16)
                peak = top[k] * SCALE
                peaks = jnp.where(lane % 8 == h, peak, peaks)
                logs = jnp.where(lane % 8 == h, peak + jnp.log(total[k]), logs)
        all_logs.append(logs)
        best = jnp.maximum(best, jnp.where(lane // 8 == doc_ref[part], peaks, NEG_BIG))

    logs = jnp.where(lane < 24, all_logs[0], all_logs[1])
    step = lane % 24 // 8
    pieces = three_parts(logs)
    tail = jnp.where(step == 0, pieces[0], jnp.where(step == 1, pieces[1], pieces[2]))
    most = three_parts(pltpu.roll(jnp.max(best, axis=0, keepdims=True), 48, 1))
    maxima = jnp.where(iota((ROWS, 128), 0) % 2 == 0, most[0], most[1])
    tail = jnp.where(lane < 48, tail, jnp.where(lane < 112, maxima, 0.0))
    out_ref[:, PARTS * WIDE :] = tail.astype(jnp.bfloat16)


def merge_kernel(got_ref, out_ref, maxima_ref):
    row = iota((ROWS, 128), 0)
    tail = got_ref[:, PARTS * WIDE :].astype(jnp.float32)

    most = tail + pltpu.roll(tail, ROWS - 1, 0)
    most = jnp.max(jnp.where(row % 2 == 0, most, NEG_BIG), axis=0, keepdims=True)
    lane_d = iota((DOCS, 128), 1)
    spread = jnp.where(lane_d // HEADS - 6 == iota((DOCS, 128), 0), most, 0.0)
    fold = as_bf16(iota((128, SPAN), 0) % HEADS == iota((128, SPAN), 1) % HEADS)
    folded = [
        jnp.dot(piece.astype(jnp.bfloat16), fold, preferred_element_type=jnp.float32)
        for piece in three_parts(spread)
    ]
    maxima_ref[...] = folded[0] + (folded[1] + folded[2])

    whole = tail + (pltpu.roll(tail, 128 - 8, 1) + pltpu.roll(tail, 128 - 16, 1))
    shift = 2 * RING
    far = pltpu.roll(pltpu.roll(whole, 128 - 24, 1), shift, 0)
    share = 1.0 / (1.0 + jnp.exp(far - whole))
    share = jnp.where(row < shift, 1.0, share)
    for h in range(HEADS):
        w = share[:, h : h + 1]
        mine = got_ref[:, h * HD : (h + 1) * HD].astype(jnp.float32)
        other = got_ref[:, WIDE + h * HD : WIDE + (h + 1) * HD].astype(jnp.float32)
        other = pltpu.roll(other, shift, 0)
        out_ref[:, h * HD : (h + 1) * HD] = (mine * w + other * (1.0 - w)).astype(jnp.bfloat16)


VMEM = pl.BlockSpec(memory_space=pltpu.VMEM)
SMEM = pl.BlockSpec(memory_space=pltpu.SMEM)
PARAMS = pltpu.CompilerParams(vmem_limit_bytes=40 * 1024 * 1024)
PREPARE_COST = pl.CostEstimate(flops=10**10, bytes_accessed=10**8, transcendentals=0)


def body(queries, keys, values, doc_lengths, source_row):
    along_ring = [[r * RING + z for z in range(RING)] for r in range(RINGS)]

    def exchange(x, groups):
        return lax.all_to_all(
            x, "ctx", split_axis=0, concat_axis=0, tiled=True, axis_index_groups=groups
        )

    own = jnp.pad(keys, ((0, 0), (0, HD))) + jnp.pad(values, ((0, 0), (HD, 0)))
    before = lax.ppermute(own, "ctx", [(c, c + RING) for c in range(CTX - RING)])
    next_queries = lax.ppermute(queries, "ctx", [(c + RING, c) for c in range(CTX - RING)])
    later = jnp.arange(RING, dtype=jnp.int32) > lax.axis_index("ctx") % RING
    slots = jnp.where(later[:, None, None], own[None], before[None])
    window = exchange(slots, along_ring).reshape(FAR, 2 * HD)
    q_rows, bias, doc = pl.pallas_call(
        prepare_kernel,
        out_shape=(
            jax.ShapeDtypeStruct((PARTS, HEADS * ROWS, HD), jnp.bfloat16),
            jax.ShapeDtypeStruct((PARTS, ROWS, WINDOW), jnp.float32),
            jax.ShapeDtypeStruct((PARTS, ROWS, 128), jnp.int32),
        ),
        in_specs=[SMEM, VMEM, VMEM, VMEM],
        out_specs=(VMEM, VMEM, VMEM),
        compiler_params=PARAMS,
        name="prepare",
    )(doc_lengths, source_row, queries, next_queries)
    wide = PARTS * WIDE + 128
    sent = pl.pallas_call(
        attend_kernel,
        out_shape=jax.ShapeDtypeStruct((ROWS, wide), jnp.bfloat16),
        in_specs=[VMEM, VMEM, VMEM, VMEM, VMEM],
        out_specs=VMEM,
        compiler_params=PARAMS,
        name="attend",
    )(q_rows, bias, doc, window, own)
    got = lax.all_to_all(
        sent.reshape(CTX, 2, wide), "ctx", split_axis=0, concat_axis=0, tiled=True
    )
    context, maxima = pl.pallas_call(
        merge_kernel,
        out_shape=(
            jax.ShapeDtypeStruct((ROWS, WIDE), jnp.bfloat16),
            jax.ShapeDtypeStruct((DOCS, SPAN), jnp.float32),
        ),
        in_specs=[VMEM],
        out_specs=(VMEM, VMEM),
        compiler_params=PARAMS,
        name="merge",
    )(got.reshape(ROWS, wide))
    head = lax.axis_index("head")
    owner = lax.broadcasted_iota(jnp.int32, (DOCS, SPAN), 1) // HEADS
    everyone = maxima
    for k in range(1, GROUPS):
        moved = lax.ppermute(maxima, "head", [(i, (i + k) % GROUPS) for i in range(GROUPS)])
        everyone = jnp.where(owner == (head + GROUPS - k) % GROUPS, moved, everyone)
    return (context, everyone.T)


def solution(mesh):
    return jax.shard_map(
        body,
        mesh=mesh,
        in_specs=(P("ctx", "head"), P("ctx", "head"), P("ctx", "head"), P(), P()),
        out_specs=(P("ctx", "head"), P()),
        check_vma=False,
    )
```

time: 77 us -> 73.3 us (0.952)
  blocking collectives: 36.6 us -> 0 us
  starting transfers between devices: 13.6 us -> 30 us
  waiting for transfers between devices: 15.9 us -> 31.8 us
  other arithmetic: 0.91 us -> 2.34 us
    all_to_all x1 -> x0, blocking collectives: 26.7 us -> none  [body(): lax.all_to_all(sent.reshape(CTX, 2, 2 * PART), 'ctx', split_axis=0, conca...]
    all_to_all x1 -> x2, waiting for transfers between devices: 7.72 us -> 22.8 us  [the longest x1 16.4 us: body(): lax.all_to_all(sent.reshape(CTX, 2, wide), 'ctx', split_axis=0, concat_ax...]
    all_gather x1 -> x0, blocking collectives: 9.95 us -> none  [body(): all_maxima = lax.all_gather(maxima, 'head', axis=0, tiled=True)]
    all_to_all x1 -> x2, starting transfers between devices: 8.32 us -> 17.9 us  [the longest x1 9.67 us: body(): lax.all_to_all(sent.reshape(CTX, 2, wide), 'ctx', split_axis=0, concat_ax...]
    ppermute x0 -> x3, starting transfers between devices: none -> 6.78 us  [body(): lax.ppermute(maxima, 'head', [(i, (i + k) % GROUPS) for i in range(GROUPS)])]
    unnamed x10 -> x6, local copies, waits for them, and re-layouts: 1.45 us -> 0.01 us
    ppermute x0 -> x3, waiting for transfers between devices: none -> 0.83 us  [body(): lax.ppermute(maxima, 'head', [(i, (i + k) % GROUPS) for i in range(GROUPS)])]
    add x0 -> x1, other arithmetic: none -> 0.82 us  [body(): own = jnp.pad(keys, ((0, 0), (0, HD))) + jnp.pad(values, ((0, 0), (HD, 0)))]
  transfers between devices with their start and end apart: 3 -> 7, of which waited for: 3 -> 5; matrix products, arithmetic and copies ran while one was open for 0% -> 0% of each run, Pallas kernels for 0% -> 2%
where the time goes in v3:
time: 73.3 us; the launch traced here: 73 us
  waiting for transfers between devices  31.8 us (43%)
  starting transfers between devices  30 us (41%)
  Pallas kernels  6.91 us (9%)
  other arithmetic  2.34 us (3%)
  local copies, waits for them, and re-layouts  1.24 us (2%)
  between operations  0.75 us (1%)
    all_to_all x1, waiting for transfers between devices, body(): lax.all_to_all(sent.reshape(CTX, 2, wide), 'ctx', split_axis=0, concat_ax...  16.4 us
    all_to_all x1, starting transfers between devices, body(): lax.all_to_all(sent.reshape(CTX, 2, wide), 'ctx', split_axis=0, concat_ax...  9.67 us
    all_to_all x1, starting transfers between devices, exchange(): lax.all_to_all(x, 'ctx', split_axis=0, concat_axis=0, tiled=True, axis_in...  8.19 us
    ppermute x1, waiting for transfers between devices, body(): lax.ppermute(queries, 'ctx', [(c + RING, c) for c in range(CTX - RING)])  6.9 us
    ppermute x3, starting transfers between devices, body(): lax.ppermute(maxima, 'head', [(i, (i + k) % GROUPS) for i in range(GROUPS)])  6.78 us
    all_to_all x1, waiting for transfers between devices, exchange(): lax.all_to_all(x, 'ctx', split_axis=0, concat_axis=0, tiled=True, axis_in...  6.42 us
    pallas_call x1, Pallas kernels, body(): pl.pallas_call(attend_kernel, out_shape=jax.ShapeDtypeStruct((ROWS, wide)...  4.4 us
    ppermute x1, starting transfers between devices, body(): lax.ppermute(own, 'ctx', [(c, c + RING) for c in range(CTX - RING)])  4.03 us
  transfers between devices with their start and end apart: 7, of which 5 were waited for; matrix products, arithmetic and copies ran while one was open for 0% of the time, Pallas kernels for 2%

profile of v3, /device:TPU:1, one launch (start us, length us, event | category | flops | bytes accessed | tf_op | source)
XLA Modules:
  0.0 73.0 jit_solution(10795118237346300071)
XLA Ops:
  0.6 0.0 copy-start
  0.6 0.0 copy-start.2
  0.7 0.0 copy-start.1
  0.7 0.8 %pad_add_fusion.own_ref = bf16[128,256]{1,0:T(8,128)(2,1)S(1)} fusion(bf16[128,128]{1,0:T(8,128)(2,1)} %param.7, bf16[128,128]{1,0:T(8,128)(2,1)} %param.6), kind=kLoop, calls=%fused_computation.1 | loop fusion | flops 131072 | bytes 131072 | tf_op jit(solution)/shard_map/add | solution.py:179
  1.5 4.0 %collective-permute-start.1 = (bf16[128,256]{1,0:T(8,128)(2,1)S(1)}, bf16[128,256]{1,0:T(8,128)(2,1)S(1)}, u32[]{:S(2)}, u32[]{:S(2)}) collective-permute-start(bf16[128,256]{1,0:T(8,128)(2,1)S(1)} %pad_add_fusion.own_ref), channel_id=1, source_target_pairs={{0,32},{4,36},{8,40},{12,44},{16,48},{20,52},{24,56},{28,60},{32,6... | collective-permute-start | bytes 196616 | tf_op jit(solution)/shard_map/ppermute | solution.py:180
  5.5 1.3 %collective-permute-done.1 = bf16[128,256]{1,0:T(8,128)(2,1)S(1)} collective-permute-done((bf16[128,256]{1,0:T(8,128)(2,1)S(1)}, bf16[128,256]{1,0:T(8,128)(2,1)S(1)}, u32[]{:S(2)}, u32[]{:S(2)}) %collective-permute-start.1) | collective-permute-done | bytes 65568 | tf_op jit(solution)/shard_map/ppermute | solution.py:180
  6.8 0.9 %broadcast_select_fusion = bf16[8,128,256]{2,1,0:T(8,128)(2,1)} fusion(pred[8]{0:T(512)(128)(4,1)S(1)} %iota_compare_fusion, bf16[128,256]{1,0:T(8,128)(2,1)S(1)} %collective-permute-done.1, bf16[128,256]{1,0:T(8,128)(2,1)S(1)} %pad_add_fusion.own_ref), kind=kLoop, calls=%fused_computation | loop fusion | flops 262144 | bytes 655368 | tf_op jit(solution)/shard_map/jit(_where)/select_n | solution.py:183
  7.7 8.2 %all-to-all-start = ((bf16[8,128,256]{2,1,0:T(8,128)(2,1)}), bf16[8,128,256]{2,1,0:T(8,128)(2,1)S(1)}, u32[]{:S(2)}, u32[]{:S(2)}) async-start(bf16[8,128,256]{2,1,0:T(8,128)(2,1)} %broadcast_select_fusion), calls=%async_computation | async-start | bytes 1048576 | tf_op jit(solution)/shard_map/all_to_all | solution.py:175
  15.9 0.0 copy-done
  15.9 1.3 %collective-permute-start = (bf16[128,1024]{1,0:T(8,128)(2,1)S(1)}, bf16[128,1024]{1,0:T(8,128)(2,1)S(1)}, u32[]{:S(2)}, u32[]{:S(2)}) collective-permute-start(bf16[128,1024]{1,0:T(8,128)(2,1)S(1)} %copy-done), channel_id=1, source_target_pairs={{32,0},{36,4},{40,8},{44,12},{48,16},{52,20},{56,24},{60,28},{64,3... | collective-permute-start | bytes 786440 | tf_op jit(solution)/shard_map/ppermute | solution.py:181
  17.2 6.9 %collective-permute-done.q1_ref = bf16[128,1024]{1,0:T(8,128)(2,1)S(1)} collective-permute-done((bf16[128,1024]{1,0:T(8,128)(2,1)S(1)}, bf16[128,1024]{1,0:T(8,128)(2,1)S(1)}, u32[]{:S(2)}, u32[]{:S(2)}) %collective-permute-start) | collective-permute-done | bytes 262176 | tf_op jit(solution)/shard_map/ppermute | solution.py:181
  24.1 0.0 copy-done.2
  24.1 0.0 copy-done.1
  24.1 1.3 %prepare.1 = (bf16[2,1024,128]{2,1,0:T(8,128)(2,1)S(1)}, f32[2,128,1152]{2,1,0:T(8,128)S(1)}, s32[2,128,128]{2,1,0:T(8,128)S(1)}) custom-call(s32[8]{0:T(128)S(1)} %copy-done.2, s32[64,128]{1,0:T(8,128)S(1)} %copy-done.1, bf16[128,1024]{1,0:T(8,128)(2,1)S(1)} %copy-done, bf16[128,1024]{1,0:T(8,128)(2,1)S(1)} %collective-permute-done.q1_ref), custom_call_target="tpu_custom_call" | custom-call | tf_op jit(solution)/shard_map/prepare/pallas_call | solution.py:185
  25.4 6.4 %all-to-all-done = bf16[8,128,256]{2,1,0:T(8,128)(2,1)S(1)} async-done(((bf16[8,128,256]{2,1,0:T(8,128)(2,1)}), bf16[8,128,256]{2,1,0:T(8,128)(2,1)S(1)}, u32[]{:S(2)}, u32[]{:S(2)}) %all-to-all-start) | async-done | bytes 524320 | tf_op jit(solution)/shard_map/all_to_all | solution.py:175
  31.9 4.4 %attend.1 = bf16[128,2176]{1,0:T(8,128)(2,1)S(1)} custom-call(bf16[2,1024,128]{2,1,0:T(8,128)(2,1)S(1)} %get-tuple-element.7.q_ref, f32[2,128,1152]{2,1,0:T(8,128)S(1)} %get-tuple-element.8.bias_ref, s32[2,128,128]{2,1,0:T(8,128)S(1)} %get-tuple-element.9.doc_ref, bf16[1024,256]{1,0:T(8,128)(2,1)S(1)} %bitcast.3, bf16[128,256]{1,0:T(8,128)(2,1)S(1)} %pad_add_fusion.own_ref), custom_call_target="tpu_custom_call" | custom-call | tf_op jit(solution)/shard_map/attend/pallas_call | solution.py:198
  36.3 1.0 %reshape.20 = bf16[64,2,2176]{2,1,0:T(2,128)(2,1)} reshape(bf16[128,2176]{1,0:T(8,128)(2,1)S(1)} %attend.1) | data formatting | bytes 1114112 | tf_op jit(solution)/shard_map/reshape | solution.py:207
  37.3 9.7 %all-to-all-start.1 = ((bf16[64,2,2176]{2,1,0:T(2,128)(2,1)}), bf16[64,2,2176]{2,1,0:T(2,128)(2,1)S(1)}, u32[]{:S(2)}, u32[]{:S(2)}) async-start(bf16[64,2,2176]{2,1,0:T(2,128)(2,1)} %reshape.20), calls=%async_computation.1 | async-start | bytes 1114112 | tf_op jit(solution)/shard_map/all_to_all | solution.py:206
  47.0 16.4 %all-to-all-done.1 = bf16[64,2,2176]{2,1,0:T(2,128)(2,1)S(1)} async-done(((bf16[64,2,2176]{2,1,0:T(2,128)(2,1)}), bf16[64,2,2176]{2,1,0:T(2,128)(2,1)S(1)}, u32[]{:S(2)}, u32[]{:S(2)}) %all-to-all-start.1) | async-done | bytes 557088 | tf_op jit(solution)/shard_map/all_to_all | solution.py:206
  63.4 0.2 reshape.21.got_ref
  63.6 1.2 %merge.1 = (bf16[128,1024]{1,0:T(8,128)(2,1)}, f32[8,32]{1,0:T(8,128)S(1)}) custom-call(bf16[128,2176]{1,0:T(8,128)(2,1)S(1)} %reshape.21.got_ref), custom_call_target="tpu_custom_call" | custom-call | tf_op jit(solution)/shard_map/merge/pallas_call | solution.py:209
  64.8 5.2 %collective-permute-start.2 = (f32[8,32]{1,0:T(8,128)S(1)}, f32[8,32]{1,0:T(8,128)S(1)}, u32[]{:S(2)}, u32[]{:S(2)}) collective-permute-start(f32[8,32]{1,0:T(8,128)S(1)} %get-tuple-element.11), channel_id=1, source_target_pairs={{0,3},{1,0},{2,1},{3,2},{4,7},{5,4},{6,5},{7,6},{8,11},{9,8},{10,9... | collective-permute-start | bytes 3080 | tf_op jit(solution)/shard_map/ppermute | solution.py:224
  70.0 0.3 collective-permute-start.3
  70.3 1.3 %collective-permute-start.4 = (f32[8,32]{1,0:T(8,128)S(1)}, f32[8,32]{1,0:T(8,128)S(1)}, u32[]{:S(2)}, u32[]{:S(2)}) collective-permute-start(f32[8,32]{1,0:T(8,128)S(1)} %get-tuple-element.11), channel_id=1, source_target_pairs={{0,1},{1,2},{2,3},{3,0},{4,5},{5,6},{6,7},{7,4},{8,9},{9,10},{10,1... | collective-permute-start | bytes 3080 | tf_op jit(solution)/shard_map/ppermute | solution.py:224
  71.6 0.0 collective-permute-done.2
  71.6 0.8 %collective-permute-done.3 = f32[8,32]{1,0:T(8,128)S(1)} collective-permute-done((f32[8,32]{1,0:T(8,128)S(1)}, f32[8,32]{1,0:T(8,128)S(1)}, u32[]{:S(2)}, u32[]{:S(2)}) %collective-permute-start.3) | collective-permute-done | bytes 1056 | tf_op jit(solution)/shard_map/ppermute | solution.py:224
  72.4 0.0 collective-permute-done.4
  72.4 0.6 select_bitcast_fusion
  (3 shorter events, 0.0 us)
Async XLA Ops:
  0.6 15.3 %copy-start = (bf16[128,1024]{1,0:T(8,128)(2,1)S(1)}, bf16[128,1024]{1,0:T(8,128)(2,1)}, u32[]{:S(2)}) copy-start(bf16[128,1024]{1,0:T(8,128)(2,1)} %q0_ref.1) | copy-start | bytes 786436
  0.6 23.5 %copy-start.2 = (s32[8]{0:T(128)S(1)}, s32[8]{0:T(128)}, u32[]{:S(2)}) copy-start(s32[8]{0:T(128)} %lengths_ref.1) | copy-start | bytes 100
  0.7 23.5 %copy-start.1 = (s32[64,128]{1,0:T(8,128)S(1)}, s32[64,128]{1,0:T(8,128)}, u32[]{:S(2)}) copy-start(s32[64,128]{1,0:T(8,128)} %source_ref.1) | copy-start | bytes 98308
  1.5 5.3 %collective-permute-start.1 = (bf16[128,256]{1,0:T(8,128)(2,1)S(1)}, bf16[128,256]{1,0:T(8,128)(2,1)S(1)}, u32[]{:S(2)}, u32[]{:S(2)}) collective-permute-start(bf16[128,256]{1,0:T(8,128)(2,1)S(1)} %pad_add_fusion.own_ref), channel_id=1, source_target_pairs={{0,32},{4,36},{8,40},{12,44},{16,48},{20,52},{24,56},{28,60},{32,6... | collective-permute-start | bytes 196616 | tf_op jit(solution)/shard_map/ppermute | solution.py:180
  7.7 24.1 %all-to-all-start = ((bf16[8,128,256]{2,1,0:T(8,128)(2,1)}), bf16[8,128,256]{2,1,0:T(8,128)(2,1)S(1)}, u32[]{:S(2)}, u32[]{:S(2)}) async-start(bf16[8,128,256]{2,1,0:T(8,128)(2,1)} %broadcast_select_fusion), calls=%async_computation | async-start | bytes 1048576 | tf_op jit(solution)/shard_map/all_to_all | solution.py:175
  15.9 8.2 %collective-permute-start = (bf16[128,1024]{1,0:T(8,128)(2,1)S(1)}, bf16[128,1024]{1,0:T(8,128)(2,1)S(1)}, u32[]{:S(2)}, u32[]{:S(2)}) collective-permute-start(bf16[128,1024]{1,0:T(8,128)(2,1)S(1)} %copy-done), channel_id=1, source_target_pairs={{32,0},{36,4},{40,8},{44,12},{48,16},{52,20},{56,24},{60,28},{64,3... | collective-permute-start | bytes 786440 | tf_op jit(solution)/shard_map/ppermute | solution.py:181
  37.3 26.1 %all-to-all-start.1 = ((bf16[64,2,2176]{2,1,0:T(2,128)(2,1)}), bf16[64,2,2176]{2,1,0:T(2,128)(2,1)S(1)}, u32[]{:S(2)}, u32[]{:S(2)}) async-start(bf16[64,2,2176]{2,1,0:T(2,128)(2,1)} %reshape.20), calls=%async_computation.1 | async-start | bytes 1114112 | tf_op jit(solution)/shard_map/all_to_all | solution.py:206
  64.8 6.8 %collective-permute-start.2 = (f32[8,32]{1,0:T(8,128)S(1)}, f32[8,32]{1,0:T(8,128)S(1)}, u32[]{:S(2)}, u32[]{:S(2)}) collective-permute-start(f32[8,32]{1,0:T(8,128)S(1)} %get-tuple-element.11), channel_id=1, source_target_pairs={{0,3},{1,0},{2,1},{3,2},{4,7},{5,4},{6,5},{7,6},{8,11},{9,8},{10,9... | collective-permute-start | bytes 3080 | tf_op jit(solution)/shard_map/ppermute | solution.py:224
  70.0 2.5 %collective-permute-start.3 = (f32[8,32]{1,0:T(8,128)S(1)}, f32[8,32]{1,0:T(8,128)S(1)}, u32[]{:S(2)}, u32[]{:S(2)}) collective-permute-start(f32[8,32]{1,0:T(8,128)S(1)} %get-tuple-element.11), channel_id=1, source_target_pairs={{0,2},{1,3},{2,0},{3,1},{4,6},{5,7},{6,4},{7,5},{8,10},{9,11},{10,... | collective-permute-start | bytes 3080 | tf_op jit(solution)/shard_map/ppermute | solution.py:224
  70.3 2.1 %collective-permute-start.4 = (f32[8,32]{1,0:T(8,128)S(1)}, f32[8,32]{1,0:T(8,128)S(1)}, u32[]{:S(2)}, u32[]{:S(2)}) collective-permute-start(f32[8,32]{1,0:T(8,128)S(1)} %get-tuple-element.11), channel_id=1, source_target_pairs={{0,1},{1,2},{2,3},{3,0},{4,5},{5,6},{6,7},{7,4},{8,9},{9,10},{10,1... | collective-permute-start | bytes 3080 | tf_op jit(solution)/shard_map/ppermute | solution.py:224

commit v4 on v3

--- a/solution.py
+++ b/solution.py
@@ -75,43 +75,45 @@
             start = jnp.where(passed, end, start)
             doc = doc + passed.astype(jnp.int32)
         doc_out[part] = jnp.broadcast_to(doc, (ROWS, 128))
-        for j in range(RING + 1):
-            block = me if j == RING else base + j - jnp.where(j >= in_ring, RING, 0)
+        for j in range(RING + part):
+            if j == RING:
+                block = me
+            else:
+                block = base + j - jnp.where(j + part > in_ring, RING, 0)
             key_pos = block * ROWS + lane
             ok = (key_pos >= start) & (key_pos <= pos)
-            if part == 0:
-                ok = ok & (block > me - RING)
             bias_out[part, :, j * 128 : (j + 1) * 128] = jnp.where(ok, 0.0, NEG_BIG)
 
 
-def attend_kernel(q_ref, bias_ref, doc_ref, kv_ref, own_ref, out_ref):
+def attend_kernel(q_ref, bias_ref, doc_ref, kv_ref, own_ref, out_ref, kv_scr):
     lane = iota((ROWS, 128), 1)
     n = HEADS_AT_ONCE
+    kv_scr[...] = kv_ref[...]
+    kv_scr[pl.ds(pl.multiple_of(lax.axis_index("ctx") % RING * ROWS, ROWS), ROWS), :] = own_ref[...]
     all_logs = []
     best = jnp.full((ROWS, 128), NEG_BIG, jnp.float32)
     for part in range(PARTS):
         peaks = jnp.full((ROWS, 128), NEG_BIG, jnp.float32)
         logs = jnp.full((ROWS, 128), NEG_BIG, jnp.float32)
+        sources = [(kv_scr, 0, FAR)] if part == 0 else [(kv_ref, 0, FAR), (own_ref, FAR, WINDOW)]
         for h0 in range(0, HEADS, n):
             q = q_ref[part, h0 * ROWS : (h0 + n) * ROWS, :]
-            s_far = dot_nt(q, kv_ref[:, :HD]).reshape(n, ROWS, FAR) + bias_ref[part, :, :FAR][None]
-            s_own = (
-                dot_nt(q, own_ref[:, :HD]).reshape(n, ROWS, ROWS) + bias_ref[part, :, FAR:][None]
-            )
-            top = jnp.maximum(
-                jnp.max(s_far, axis=2, keepdims=True), jnp.max(s_own, axis=2, keepdims=True)
-            )
-            w_far = jnp.exp2((s_far - top) * SCALE_LOG2E)
-            w_own = jnp.exp2((s_own - top) * SCALE_LOG2E)
-            total = jnp.sum(w_far, axis=2, keepdims=True) + jnp.sum(w_own, axis=2, keepdims=True)
-            acc = jnp.dot(
-                w_far.astype(jnp.bfloat16).reshape(n * ROWS, FAR),
-                kv_ref[:, HD:],
-                preferred_element_type=jnp.float32,
-            ) + jnp.dot(
-                w_own.astype(jnp.bfloat16).reshape(n * ROWS, ROWS),
-                own_ref[:, HD:],
-                preferred_element_type=jnp.float32,
+            scores = [
+                dot_nt(q, ref[:, :HD]).reshape(n, ROWS, high - low)
+                + bias_ref[part, :, low:high][None]
+                for ref, low, high in sources
+            ]
+            tops = [jnp.max(s, axis=2, keepdims=True) for s in scores]
+            top = tops[0] if part == 0 else jnp.maximum(tops[0], tops[1])
+            weights = [jnp.exp2((s - top) * SCALE_LOG2E) for s in scores]
+            total = sum(jnp.sum(w, axis=2, keepdims=True) for w in weights)
+            acc = sum(
+                jnp.dot(
+                    w.astype(jnp.bfloat16).reshape(n * ROWS, high - low),
+                    ref[:, HD:],
+                    preferred_element_type=jnp.float32,
+                )
+                for w, (ref, low, high) in zip(weights, sources)
             )
             context = acc.reshape(n, ROWS, HD) / total
             for k in range(n):
@@ -134,9 +136,9 @@
     out_ref[:, PARTS * WIDE :] = tail.astype(jnp.bfloat16)
 
 
-def merge_kernel(got_ref, out_ref, maxima_ref):
+def maxima_kernel(tail_ref, maxima_ref):
     row = iota((ROWS, 128), 0)
-    tail = got_ref[:, PARTS * WIDE :].astype(jnp.float32)
+    tail = tail_ref[:, PARTS * WIDE :].astype(jnp.float32)
 
     most = tail + pltpu.roll(tail, ROWS - 1, 0)
     most = jnp.max(jnp.where(row % 2 == 0, most, NEG_BIG), axis=0, keepdims=True)
@@ -147,7 +149,13 @@
         jnp.dot(piece.astype(jnp.bfloat16), fold, preferred_element_type=jnp.float32)
         for piece in three_parts(spread)
     ]
-    maxima_ref[...] = folded[0] + (folded[1] + folded[2])
+    mine = iota((DOCS, SPAN), 1) // HEADS == lax.axis_index("head")
+    maxima_ref[...] = jnp.where(mine, folded[0] + (folded[1] + folded[2]), 0.0)
+
+
+def merge_kernel(got_ref, out_ref):
+    row = iota((ROWS, 128), 0)
+    tail = got_ref[:, PARTS * WIDE :].astype(jnp.float32)
 
     whole = tail + (pltpu.roll(tail, 128 - 8, 1) + pltpu.roll(tail, 128 - 16, 1))
     shift = 2 * RING
@@ -165,7 +173,7 @@
 VMEM = pl.BlockSpec(memory_space=pltpu.VMEM)
 SMEM = pl.BlockSpec(memory_space=pltpu.SMEM)
 PARAMS = pltpu.CompilerParams(vmem_limit_bytes=40 * 1024 * 1024)
-PREPARE_COST = pl.CostEstimate(flops=10**10, bytes_accessed=10**8, transcendentals=0)
+MERGE_COST = pl.CostEstimate(flops=10**8, bytes_accessed=10**7, transcendentals=0)
 
 
 def body(queries, keys, values, doc_lengths, source_row):
@@ -200,29 +208,36 @@
         out_shape=jax.ShapeDtypeStruct((ROWS, wide), jnp.bfloat16),
         in_specs=[VMEM, VMEM, VMEM, VMEM, VMEM],
         out_specs=VMEM,
+        scratch_shapes=[pltpu.VMEM((FAR, 2 * HD), jnp.bfloat16)],
         compiler_params=PARAMS,
         name="attend",
     )(q_rows, bias, doc, window, own)
     got = lax.all_to_all(
         sent.reshape(CTX, 2, wide), "ctx", split_axis=0, concat_axis=0, tiled=True
     )
-    context, maxima = pl.pallas_call(
-        merge_kernel,
-        out_shape=(
-            jax.ShapeDtypeStruct((ROWS, WIDE), jnp.bfloat16),
-            jax.ShapeDtypeStruct((DOCS, SPAN), jnp.float32),
-        ),
+    got = got.reshape(ROWS, wide)
+    maxima = pl.pallas_call(
+        maxima_kernel,
+        out_shape=jax.ShapeDtypeStruct((DOCS, SPAN), jnp.float32),
         in_specs=[VMEM],
-        out_specs=(VMEM, VMEM),
-        compiler_params=PARAMS,
-        name="merge",
-    )(got.reshape(ROWS, wide))
-    head = lax.axis_index("head")
-    owner = lax.broadcasted_iota(jnp.int32, (DOCS, SPAN), 1) // HEADS
+        out_specs=VMEM,
+        compiler_params=PARAMS,
+        name="maxima",
+    )(got)
     everyone = maxima
     for k in range(1, GROUPS):
-        moved = lax.ppermute(maxima, "head", [(i, (i + k) % GROUPS) for i in range(GROUPS)])
-        everyone = jnp.where(owner == (head + GROUPS - k) % GROUPS, moved, everyone)
+        everyone = everyone + lax.ppermute(
+            maxima, "head", [(i, (i + k) % GROUPS) for i in range(GROUPS)]
+        )
+    context = pl.pallas_call(
+        merge_kernel,
+        out_shape=jax.ShapeDtypeStruct((ROWS, WIDE), jnp.bfloat16),
+        in_specs=[VMEM],
+        out_specs=VMEM,
+        cost_estimate=MERGE_COST,
+        compiler_params=PARAMS,
+        name="merge",
+    )(got)
     return (context, everyone.T)
 
 

time: 73.3 us -> 71.4 us (0.974)
  blocking collectives: 0 us -> 25.9 us
  waiting for transfers between devices: 31.8 us -> 14.6 us
  starting transfers between devices: 30 us -> 20.4 us
  local copies, waits for them, and re-layouts: 1.24 us -> 0.43 us
    all_to_all x0 -> x1, blocking collectives: none -> 25.9 us  [body(): lax.all_to_all(sent.reshape(CTX, 2, wide), 'ctx', split_axis=0, concat_ax...]
    all_to_all x1 -> x0, waiting for transfers between devices: 16.4 us -> none  [body(): lax.all_to_all(sent.reshape(CTX, 2, wide), 'ctx', split_axis=0, concat_ax...]
    all_to_all x1 -> x0, starting transfers between devices: 9.67 us -> none  [body(): lax.all_to_all(sent.reshape(CTX, 2, wide), 'ctx', split_axis=0, concat_ax...]
    ppermute x3, waiting for transfers between devices: 0.83 us -> 0.01 us  [body(): lax.ppermute(maxima, 'head', [(i, (i + k) % GROUPS) for i in range(GROUPS)])]
    reshape x1, local copies, waits for them, and re-layouts: 1.02 us -> 0.21 us  [body(): sent.reshape(CTX, 2, wide)]
  transfers between devices with their start and end apart: 7 -> 6, of which waited for: 5 -> 3; matrix products, arithmetic and copies ran while one was open for 0% -> 0% of each run, Pallas kernels for 2% -> 3%
where the time goes in v4:
time: 71.4 us; the launch traced here: 71.1 us
  blocking collectives  25.9 us (36%)
  starting transfers between devices  20.4 us (29%)
  waiting for transfers between devices  14.6 us (20%)
  Pallas kernels  6.72 us (9%)
  other arithmetic  2.32 us (3%)
  between operations  0.73 us (1%)
    all_to_all x1, blocking collectives, body(): lax.all_to_all(sent.reshape(CTX, 2, wide), 'ctx', split_axis=0, concat_ax...  25.9 us
    all_to_all x1, starting transfers between devices, exchange(): lax.all_to_all(x, 'ctx', split_axis=0, concat_axis=0, tiled=True, axis_in...  8.19 us
    ppermute x1, waiting for transfers between devices, body(): lax.ppermute(queries, 'ctx', [(c + RING, c) for c in range(CTX - RING)])  6.9 us
    ppermute x3, starting transfers between devices, body(): lax.ppermute(maxima, 'head', [(i, (i + k) % GROUPS) for i in range(GROUPS)])  6.87 us
    all_to_all x1, waiting for transfers between devices, exchange(): lax.all_to_all(x, 'ctx', split_axis=0, concat_axis=0, tiled=True, axis_in...  6.45 us
    pallas_call x1, Pallas kernels, body(): pl.pallas_call(attend_kernel, out_shape=jax.ShapeDtypeStruct((ROWS, wide)...  4.1 us
    ppermute x1, starting transfers between devices, body(): lax.ppermute(own, 'ctx', [(c, c + RING) for c in range(CTX - RING)])  4.03 us
  transfers between devices with their start and end apart: 6, of which 3 were waited for; matrix products, arithmetic and copies ran while one was open for 0% of the time, Pallas kernels for 3%

profile of v4, /device:TPU:1, one launch (start us, length us, event | category | flops | bytes accessed | tf_op | source)
XLA Modules:
  0.0 71.1 jit_solution(7003020536627121943)
XLA Ops:
  0.6 0.0 copy-start
  0.6 0.0 copy-start.1
  0.7 0.0 copy-start.2
  0.7 0.8 %pad_add_fusion.own_ref = bf16[128,256]{1,0:T(8,128)(2,1)S(1)} fusion(bf16[128,128]{1,0:T(8,128)(2,1)} %param.7, bf16[128,128]{1,0:T(8,128)(2,1)} %param.6), kind=kLoop, calls=%fused_computation.1 | loop fusion | flops 131072 | bytes 131072 | tf_op jit(solution)/shard_map/add | solution.py:187
  1.5 4.0 %collective-permute-start.1 = (bf16[128,256]{1,0:T(8,128)(2,1)S(1)}, bf16[128,256]{1,0:T(8,128)(2,1)S(1)}, u32[]{:S(2)}, u32[]{:S(2)}) collective-permute-start(bf16[128,256]{1,0:T(8,128)(2,1)S(1)} %pad_add_fusion.own_ref), channel_id=1, source_target_pairs={{0,32},{4,36},{8,40},{12,44},{16,48},{20,52},{24,56},{28,60},{32,6... | collective-permute-start | bytes 196616 | tf_op jit(solution)/shard_map/ppermute | solution.py:188
  5.5 1.3 %collective-permute-done.1 = bf16[128,256]{1,0:T(8,128)(2,1)S(1)} collective-permute-done((bf16[128,256]{1,0:T(8,128)(2,1)S(1)}, bf16[128,256]{1,0:T(8,128)(2,1)S(1)}, u32[]{:S(2)}, u32[]{:S(2)}) %collective-permute-start.1) | collective-permute-done | bytes 65568 | tf_op jit(solution)/shard_map/ppermute | solution.py:188
  6.8 0.9 %broadcast_select_fusion = bf16[8,128,256]{2,1,0:T(8,128)(2,1)} fusion(pred[8]{0:T(512)(128)(4,1)S(1)} %iota_compare_fusion, bf16[128,256]{1,0:T(8,128)(2,1)S(1)} %collective-permute-done.1, bf16[128,256]{1,0:T(8,128)(2,1)S(1)} %pad_add_fusion.own_ref), kind=kLoop, calls=%fused_computation | loop fusion | flops 262144 | bytes 655368 | tf_op jit(solution)/shard_map/jit(_where)/select_n | solution.py:191
  7.7 8.2 %all-to-all-start = ((bf16[8,128,256]{2,1,0:T(8,128)(2,1)}), bf16[8,128,256]{2,1,0:T(8,128)(2,1)S(1)}, u32[]{:S(2)}, u32[]{:S(2)}) async-start(bf16[8,128,256]{2,1,0:T(8,128)(2,1)} %broadcast_select_fusion), calls=%async_computation | async-start | bytes 1048576 | tf_op jit(solution)/shard_map/all_to_all | solution.py:183
  15.9 0.0 copy-done
  15.9 1.3 %collective-permute-start = (bf16[128,1024]{1,0:T(8,128)(2,1)S(1)}, bf16[128,1024]{1,0:T(8,128)(2,1)S(1)}, u32[]{:S(2)}, u32[]{:S(2)}) collective-permute-start(bf16[128,1024]{1,0:T(8,128)(2,1)S(1)} %copy-done), channel_id=1, source_target_pairs={{32,0},{36,4},{40,8},{44,12},{48,16},{52,20},{56,24},{60,28},{64,3... | collective-permute-start | bytes 786440 | tf_op jit(solution)/shard_map/ppermute | solution.py:189
  17.2 6.9 %collective-permute-done.q1_ref = bf16[128,1024]{1,0:T(8,128)(2,1)S(1)} collective-permute-done((bf16[128,1024]{1,0:T(8,128)(2,1)S(1)}, bf16[128,1024]{1,0:T(8,128)(2,1)S(1)}, u32[]{:S(2)}, u32[]{:S(2)}) %collective-permute-start) | collective-permute-done | bytes 262176 | tf_op jit(solution)/shard_map/ppermute | solution.py:189
  24.1 0.0 copy-done.1
  24.1 0.0 copy-done.2
  24.1 1.3 %prepare.1 = (bf16[2,1024,128]{2,1,0:T(8,128)(2,1)S(1)}, f32[2,128,1152]{2,1,0:T(8,128)S(1)}, s32[2,128,128]{2,1,0:T(8,128)S(1)}) custom-call(s32[8]{0:T(128)S(1)} %copy-done.2, s32[64,128]{1,0:T(8,128)S(1)} %copy-done.1, bf16[128,1024]{1,0:T(8,128)(2,1)S(1)} %copy-done, bf16[128,1024]{1,0:T(8,128)(2,1)S(1)} %collective-permute-done.q1_ref), custom_call_target="tpu_custom_call" | custom-call | tf_op jit(solution)/shard_map/prepare/pallas_call | solution.py:193
  25.4 6.4 %all-to-all-done = bf16[8,128,256]{2,1,0:T(8,128)(2,1)S(1)} async-done(((bf16[8,128,256]{2,1,0:T(8,128)(2,1)}), bf16[8,128,256]{2,1,0:T(8,128)(2,1)S(1)}, u32[]{:S(2)}, u32[]{:S(2)}) %all-to-all-start) | async-done | bytes 524320 | tf_op jit(solution)/shard_map/all_to_all | solution.py:183
  31.9 4.1 %attend.1 = bf16[128,2176]{1,0:T(8,128)(2,1)S(1)} custom-call(bf16[2,1024,128]{2,1,0:T(8,128)(2,1)S(1)} %get-tuple-element.5.q_ref, f32[2,128,1152]{2,1,0:T(8,128)S(1)} %get-tuple-element.6.bias_ref, s32[2,128,128]{2,1,0:T(8,128)S(1)} %get-tuple-element.7.doc_ref, bf16[1024,256]{1,0:T(8,128)(2,1)S(1)} %bitcast.3, bf16[128,256]{1,0:T(8,128)(2,1)S(1)} %pad_add_fusion.own_ref), custom_call_target="tpu_custom_call" | custom-call | tf_op jit(solution)/shard_map/attend/pallas_call | solution.py:206
  36.0 0.2 reshape.20
  36.2 25.9 %all_to_all.10 = bf16[64,2,2176]{2,1,0:T(2,128)(2,1)S(1)} all-to-all(bf16[64,2,2176]{2,1,0:T(2,128)(2,1)S(1)} %reshape.20), channel_id=1, replica_groups=mesh['ctx'=64,'head'=4] {'ctx'}, dimensions={0} | all-to-all | bytes 1114112 | tf_op jit(solution)/shard_map/all_to_all | solution.py:215
  62.1 0.2 reshape.21.got_ref.tail_ref
  62.3 0.2 maxima.1
  62.5 5.2 %collective-permute-start.4 = (f32[8,32]{1,0:T(8,128)S(1)}, f32[8,32]{1,0:T(8,128)S(1)}, u32[]{:S(2)}, u32[]{:S(2)}) collective-permute-start(f32[8,32]{1,0:T(8,128)S(1)} %maxima.1), channel_id=1, source_target_pairs={{0,3},{1,0},{2,1},{3,2},{4,7},{5,4},{6,5},{7,6},{8,11},{9,8},{10,9... | collective-permute-start | bytes 3080 | tf_op jit(solution)/shard_map/ppermute | solution.py:229
  67.6 0.3 collective-permute-start.3
  68.0 1.4 %collective-permute-start.2 = (f32[8,32]{1,0:T(8,128)S(1)}, f32[8,32]{1,0:T(8,128)S(1)}, u32[]{:S(2)}, u32[]{:S(2)}) collective-permute-start(f32[8,32]{1,0:T(8,128)S(1)} %maxima.1), channel_id=1, source_target_pairs={{0,1},{1,2},{2,3},{3,0},{4,5},{5,6},{6,7},{7,4},{8,9},{9,10},{10,1... | collective-permute-start | bytes 3080 | tf_op jit(solution)/shard_map/ppermute | solution.py:229
  69.3 1.2 %merge.1 = bf16[128,1024]{1,0:T(8,128)(2,1)} custom-call(bf16[128,2176]{1,0:T(8,128)(2,1)S(1)} %reshape.21.got_ref.tail_ref), custom_call_target="tpu_custom_call" | custom-call | flops 100000000 | bytes 10000000 | tf_op jit(solution)/shard_map/merge/pallas_call | solution.py:232
  70.5 0.0 collective-permute-done.4
  70.5 0.0 collective-permute-done.3
  70.5 0.0 collective-permute-done.2
  70.5 0.6 add_bitcast_fusion
  (1 shorter events, 0.0 us)
Async XLA Ops:
  0.6 15.3 %copy-start = (bf16[128,1024]{1,0:T(8,128)(2,1)S(1)}, bf16[128,1024]{1,0:T(8,128)(2,1)}, u32[]{:S(2)}) copy-start(bf16[128,1024]{1,0:T(8,128)(2,1)} %q0_ref.1) | copy-start | bytes 786436
  0.6 23.5 %copy-start.1 = (s32[64,128]{1,0:T(8,128)S(1)}, s32[64,128]{1,0:T(8,128)}, u32[]{:S(2)}) copy-start(s32[64,128]{1,0:T(8,128)} %source_ref.1) | copy-start | bytes 98308
  0.7 23.5 %copy-start.2 = (s32[8]{0:T(128)S(1)}, s32[8]{0:T(128)}, u32[]{:S(2)}) copy-start(s32[8]{0:T(128)} %lengths_ref.1) | copy-start | bytes 100
  1.5 5.3 %collective-permute-start.1 = (bf16[128,256]{1,0:T(8,128)(2,1)S(1)}, bf16[128,256]{1,0:T(8,128)(2,1)S(1)}, u32[]{:S(2)}, u32[]{:S(2)}) collective-permute-start(bf16[128,256]{1,0:T(8,128)(2,1)S(1)} %pad_add_fusion.own_ref), channel_id=1, source_target_pairs={{0,32},{4,36},{8,40},{12,44},{16,48},{20,52},{24,56},{28,60},{32,6... | collective-permute-start | bytes 196616 | tf_op jit(solution)/shard_map/ppermute | solution.py:188
  7.7 24.1 %all-to-all-start = ((bf16[8,128,256]{2,1,0:T(8,128)(2,1)}), bf16[8,128,256]{2,1,0:T(8,128)(2,1)S(1)}, u32[]{:S(2)}, u32[]{:S(2)}) async-start(bf16[8,128,256]{2,1,0:T(8,128)(2,1)} %broadcast_select_fusion), calls=%async_computation | async-start | bytes 1048576 | tf_op jit(solution)/shard_map/all_to_all | solution.py:183
  15.9 8.2 %collective-permute-start = (bf16[128,1024]{1,0:T(8,128)(2,1)S(1)}, bf16[128,1024]{1,0:T(8,128)(2,1)S(1)}, u32[]{:S(2)}, u32[]{:S(2)}) collective-permute-start(bf16[128,1024]{1,0:T(8,128)(2,1)S(1)} %copy-done), channel_id=1, source_target_pairs={{32,0},{36,4},{40,8},{44,12},{48,16},{52,20},{56,24},{60,28},{64,3... | collective-permute-start | bytes 786440 | tf_op jit(solution)/shard_map/ppermute | solution.py:189
  62.5 8.1 %collective-permute-start.4 = (f32[8,32]{1,0:T(8,128)S(1)}, f32[8,32]{1,0:T(8,128)S(1)}, u32[]{:S(2)}, u32[]{:S(2)}) collective-permute-start(f32[8,32]{1,0:T(8,128)S(1)} %maxima.1), channel_id=1, source_target_pairs={{0,3},{1,0},{2,1},{3,2},{4,7},{5,4},{6,5},{7,6},{8,11},{9,8},{10,9... | collective-permute-start | bytes 3080 | tf_op jit(solution)/shard_map/ppermute | solution.py:229
  67.6 2.9 %collective-permute-start.3 = (f32[8,32]{1,0:T(8,128)S(1)}, f32[8,32]{1,0:T(8,128)S(1)}, u32[]{:S(2)}, u32[]{:S(2)}) collective-permute-start(f32[8,32]{1,0:T(8,128)S(1)} %maxima.1), channel_id=1, source_target_pairs={{0,2},{1,3},{2,0},{3,1},{4,6},{5,7},{6,4},{7,5},{8,10},{9,11},{10,... | collective-permute-start | bytes 3080 | tf_op jit(solution)/shard_map/ppermute | solution.py:229
  68.0 2.6 %collective-permute-start.2 = (f32[8,32]{1,0:T(8,128)S(1)}, f32[8,32]{1,0:T(8,128)S(1)}, u32[]{:S(2)}, u32[]{:S(2)}) collective-permute-start(f32[8,32]{1,0:T(8,128)S(1)} %maxima.1), channel_id=1, source_target_pairs={{0,1},{1,2},{2,3},{3,0},{4,5},{5,6},{6,7},{7,4},{8,9},{9,10},{10,1... | collective-permute-start | bytes 3080 | tf_op jit(solution)/shard_map/ppermute | solution.py:229

commit v5 on v4

--- a/solution.py
+++ b/solution.py
@@ -22,7 +22,7 @@
 NEG_BIG = -1e30
 SCALE = 1.0 / math.sqrt(HD)
 SCALE_LOG2E = SCALE * math.log2(math.e)
-HEADS_AT_ONCE = 4
+HEADS_AT_ONCE = 2
 SPAN = GROUPS * HEADS
 
 
@@ -90,41 +90,46 @@
     n = HEADS_AT_ONCE
     kv_scr[...] = kv_ref[...]
     kv_scr[pl.ds(pl.multiple_of(lax.axis_index("ctx") % RING * ROWS, ROWS), ROWS), :] = own_ref[...]
-    all_logs = []
+    all_peaks = [jnp.full((ROWS, 128), NEG_BIG, jnp.float32)] * PARTS
+    all_logs = [jnp.full((ROWS, 128), NEG_BIG, jnp.float32)] * PARTS
+    sources = [[(kv_scr, 0, FAR)], [(kv_ref, 0, FAR), (own_ref, FAR, WINDOW)]]
+
+    def scores_of(part, h0):
+        q = q_ref[part, h0 * ROWS : (h0 + n) * ROWS, :]
+        return [
+            dot_nt(q, ref[:, :HD]).reshape(n, ROWS, high - low) + bias_ref[part, :, low:high][None]
+            for ref, low, high in sources[part]
+        ]
+
+    jobs = [(part, h0) for part in range(PARTS) for h0 in range(0, HEADS, n)]
+    ahead = scores_of(*jobs[0])
+    for i, (part, h0) in enumerate(jobs):
+        scores = ahead
+        if i + 1 < len(jobs):
+            ahead = scores_of(*jobs[i + 1])
+        tops = [jnp.max(s, axis=2, keepdims=True) for s in scores]
+        top = tops[0] if part == 0 else jnp.maximum(tops[0], tops[1])
+        weights = [jnp.exp2((s - top) * SCALE_LOG2E) for s in scores]
+        total = sum(jnp.sum(w, axis=2, keepdims=True) for w in weights)
+        acc = sum(
+            jnp.dot(
+                w.astype(jnp.bfloat16).reshape(n * ROWS, high - low),
+                ref[:, HD:],
+                preferred_element_type=jnp.float32,
+            )
+            for w, (ref, low, high) in zip(weights, sources[part])
+        )
+        context = acc.reshape(n, ROWS, HD) * (1.0 / total)
+        for k in range(n):
+            h = h0 + k
+            at = part * WIDE + h * HD
+            out_ref[:, at : at + HD] = context[k].astype(jnp.bfloat16)
+            peak = top[k] * SCALE
+            all_peaks[part] = jnp.where(lane % 8 == h, peak, all_peaks[part])
+            all_logs[part] = jnp.where(lane % 8 == h, peak + jnp.log(total[k]), all_logs[part])
     best = jnp.full((ROWS, 128), NEG_BIG, jnp.float32)
     for part in range(PARTS):
-        peaks = jnp.full((ROWS, 128), NEG_BIG, jnp.float32)
-        logs = jnp.full((ROWS, 128), NEG_BIG, jnp.float32)
-        sources = [(kv_scr, 0, FAR)] if part == 0 else [(kv_ref, 0, FAR), (own_ref, FAR, WINDOW)]
-        for h0 in range(0, HEADS, n):
-            q = q_ref[part, h0 * ROWS : (h0 + n) * ROWS, :]
-            scores = [
-                dot_nt(q, ref[:, :HD]).reshape(n, ROWS, high - low)
-                + bias_ref[part, :, low:high][None]
-                for ref, low, high in sources
-            ]
-            tops = [jnp.max(s, axis=2, keepdims=True) for s in scores]
-            top = tops[0] if part == 0 else jnp.maximum(tops[0], tops[1])
-            weights = [jnp.exp2((s - top) * SCALE_LOG2E) for s in scores]
-            total = sum(jnp.sum(w, axis=2, keepdims=True) for w in weights)
-            acc = sum(
-                jnp.dot(
-                    w.astype(jnp.bfloat16).reshape(n * ROWS, high - low),
-                    ref[:, HD:],
-                    preferred_element_type=jnp.float32,
-                )
-                for w, (ref, low, high) in zip(weights, sources)
-            )
-            context = acc.reshape(n, ROWS, HD) / total
-            for k in range(n):
-                h = h0 + k
-                at = part * WIDE + h * HD
-                out_ref[:, at : at + HD] = context[k].astype(jnp.bfloat16)
-                peak = top[k] * SCALE
-                peaks = jnp.where(lane % 8 == h, peak, peaks)
-                logs = jnp.where(lane % 8 == h, peak + jnp.log(total[k]), logs)
-        all_logs.append(logs)
-        best = jnp.maximum(best, jnp.where(lane // 8 == doc_ref[part], peaks, NEG_BIG))
+        best = jnp.maximum(best, jnp.where(lane // 8 == doc_ref[part], all_peaks[part], NEG_BIG))
 
     logs = jnp.where(lane < 24, all_logs[0], all_logs[1])
     step = lane % 24 // 8

time: 71.4 us -> 70.9 us (level)
  no operation moved by 1% of the time
where the time goes in v5:
time: 70.9 us; the launch traced here: 70.7 us
  blocking collectives  25.9 us (37%)
  starting transfers between devices  20.4 us (29%)
  waiting for transfers between devices  14.6 us (21%)
  Pallas kernels  6.24 us (9%)
  other arithmetic  2.32 us (3%)
  between operations  0.73 us (1%)
    all_to_all x1, blocking collectives, body(): lax.all_to_all(sent.reshape(CTX, 2, wide), 'ctx', split_axis=0, concat_ax...  25.9 us
    all_to_all x1, starting transfers between devices, exchange(): lax.all_to_all(x, 'ctx', split_axis=0, concat_axis=0, tiled=True, axis_in...  8.19 us
    ppermute x1, waiting for transfers between devices, body(): lax.ppermute(queries, 'ctx', [(c + RING, c) for c in range(CTX - RING)])  6.9 us
    ppermute x3, starting transfers between devices, body(): lax.ppermute(maxima, 'head', [(i, (i + k) % GROUPS) for i in range(GROUPS)])  6.87 us
    all_to_all x1, waiting for transfers between devices, exchange(): lax.all_to_all(x, 'ctx', split_axis=0, concat_axis=0, tiled=True, axis_in...  6.45 us
    ppermute x1, starting transfers between devices, body(): lax.ppermute(own, 'ctx', [(c, c + RING) for c in range(CTX - RING)])  4.03 us
    pallas_call x1, Pallas kernels, body(): pl.pallas_call(attend_kernel, out_shape=jax.ShapeDtypeStruct((ROWS, wide)...  3.62 us
  transfers between devices with their start and end apart: 6, of which 3 were waited for; matrix products, arithmetic and copies ran while one was open for 0% of the time, Pallas kernels for 3%

profile of v5, /device:TPU:1, one launch (start us, length us, event | category | flops | bytes accessed | tf_op | source)
XLA Modules:
  0.0 70.7 jit_solution(6001418801687418401)
XLA Ops:
  0.6 0.0 copy-start
  0.6 0.0 copy-start.1
  0.7 0.0 copy-start.2
  0.7 0.8 %pad_add_fusion.own_ref = bf16[128,256]{1,0:T(8,128)(2,1)S(1)} fusion(bf16[128,128]{1,0:T(8,128)(2,1)} %param.7, bf16[128,128]{1,0:T(8,128)(2,1)} %param.6), kind=kLoop, calls=%fused_computation.1 | loop fusion | flops 131072 | bytes 131072 | tf_op jit(solution)/shard_map/add | solution.py:192
  1.5 4.0 %collective-permute-start.1 = (bf16[128,256]{1,0:T(8,128)(2,1)S(1)}, bf16[128,256]{1,0:T(8,128)(2,1)S(1)}, u32[]{:S(2)}, u32[]{:S(2)}) collective-permute-start(bf16[128,256]{1,0:T(8,128)(2,1)S(1)} %pad_add_fusion.own_ref), channel_id=1, source_target_pairs={{0,32},{4,36},{8,40},{12,44},{16,48},{20,52},{24,56},{28,60},{32,6... | collective-permute-start | bytes 196616 | tf_op jit(solution)/shard_map/ppermute | solution.py:193
  5.5 1.3 %collective-permute-done.1 = bf16[128,256]{1,0:T(8,128)(2,1)S(1)} collective-permute-done((bf16[128,256]{1,0:T(8,128)(2,1)S(1)}, bf16[128,256]{1,0:T(8,128)(2,1)S(1)}, u32[]{:S(2)}, u32[]{:S(2)}) %collective-permute-start.1) | collective-permute-done | bytes 65568 | tf_op jit(solution)/shard_map/ppermute | solution.py:193
  6.8 0.9 %broadcast_select_fusion = bf16[8,128,256]{2,1,0:T(8,128)(2,1)} fusion(pred[8]{0:T(512)(128)(4,1)S(1)} %iota_compare_fusion, bf16[128,256]{1,0:T(8,128)(2,1)S(1)} %collective-permute-done.1, bf16[128,256]{1,0:T(8,128)(2,1)S(1)} %pad_add_fusion.own_ref), kind=kLoop, calls=%fused_computation | loop fusion | flops 262144 | bytes 655368 | tf_op jit(solution)/shard_map/jit(_where)/select_n | solution.py:196
  7.7 8.2 %all-to-all-start = ((bf16[8,128,256]{2,1,0:T(8,128)(2,1)}), bf16[8,128,256]{2,1,0:T(8,128)(2,1)S(1)}, u32[]{:S(2)}, u32[]{:S(2)}) async-start(bf16[8,128,256]{2,1,0:T(8,128)(2,1)} %broadcast_select_fusion), calls=%async_computation | async-start | bytes 1048576 | tf_op jit(solution)/shard_map/all_to_all | solution.py:188
  15.9 0.0 copy-done
  15.9 1.3 %collective-permute-start = (bf16[128,1024]{1,0:T(8,128)(2,1)S(1)}, bf16[128,1024]{1,0:T(8,128)(2,1)S(1)}, u32[]{:S(2)}, u32[]{:S(2)}) collective-permute-start(bf16[128,1024]{1,0:T(8,128)(2,1)S(1)} %copy-done), channel_id=1, source_target_pairs={{32,0},{36,4},{40,8},{44,12},{48,16},{52,20},{56,24},{60,28},{64,3... | collective-permute-start | bytes 786440 | tf_op jit(solution)/shard_map/ppermute | solution.py:194
  17.2 6.9 %collective-permute-done.q1_ref = bf16[128,1024]{1,0:T(8,128)(2,1)S(1)} collective-permute-done((bf16[128,1024]{1,0:T(8,128)(2,1)S(1)}, bf16[128,1024]{1,0:T(8,128)(2,1)S(1)}, u32[]{:S(2)}, u32[]{:S(2)}) %collective-permute-start) | collective-permute-done | bytes 262176 | tf_op jit(solution)/shard_map/ppermute | solution.py:194
  24.1 0.0 copy-done.1
  24.1 0.0 copy-done.2
  24.1 1.3 %prepare.1 = (bf16[2,1024,128]{2,1,0:T(8,128)(2,1)S(1)}, f32[2,128,1152]{2,1,0:T(8,128)S(1)}, s32[2,128,128]{2,1,0:T(8,128)S(1)}) custom-call(s32[8]{0:T(128)S(1)} %copy-done.2, s32[64,128]{1,0:T(8,128)S(1)} %copy-done.1, bf16[128,1024]{1,0:T(8,128)(2,1)S(1)} %copy-done, bf16[128,1024]{1,0:T(8,128)(2,1)S(1)} %collective-permute-done.q1_ref), custom_call_target="tpu_custom_call" | custom-call | tf_op jit(solution)/shard_map/prepare/pallas_call | solution.py:198
  25.4 6.4 %all-to-all-done = bf16[8,128,256]{2,1,0:T(8,128)(2,1)S(1)} async-done(((bf16[8,128,256]{2,1,0:T(8,128)(2,1)}), bf16[8,128,256]{2,1,0:T(8,128)(2,1)S(1)}, u32[]{:S(2)}, u32[]{:S(2)}) %all-to-all-start) | async-done | bytes 524320 | tf_op jit(solution)/shard_map/all_to_all | solution.py:188
  31.9 3.6 %attend.1 = bf16[128,2176]{1,0:T(8,128)(2,1)S(1)} custom-call(bf16[2,1024,128]{2,1,0:T(8,128)(2,1)S(1)} %get-tuple-element.5.q_ref, f32[2,128,1152]{2,1,0:T(8,128)S(1)} %get-tuple-element.6.bias_ref, s32[2,128,128]{2,1,0:T(8,128)S(1)} %get-tuple-element.7.doc_ref, bf16[1024,256]{1,0:T(8,128)(2,1)S(1)} %bitcast.3, bf16[128,256]{1,0:T(8,128)(2,1)S(1)} %pad_add_fusion.own_ref), custom_call_target="tpu_custom_call" | custom-call | tf_op jit(solution)/shard_map/attend/pallas_call | solution.py:211
  35.5 0.2 reshape.20
  35.7 25.9 %all_to_all.10 = bf16[64,2,2176]{2,1,0:T(2,128)(2,1)S(1)} all-to-all(bf16[64,2,2176]{2,1,0:T(2,128)(2,1)S(1)} %reshape.20), channel_id=1, replica_groups=mesh['ctx'=64,'head'=4] {'ctx'}, dimensions={0} | all-to-all | bytes 1114112 | tf_op jit(solution)/shard_map/all_to_all | solution.py:220
  61.6 0.2 reshape.21.got_ref.tail_ref
  61.8 0.2 maxima.1
  62.0 5.2 %collective-permute-start.4 = (f32[8,32]{1,0:T(8,128)S(1)}, f32[8,32]{1,0:T(8,128)S(1)}, u32[]{:S(2)}, u32[]{:S(2)}) collective-permute-start(f32[8,32]{1,0:T(8,128)S(1)} %maxima.1), channel_id=1, source_target_pairs={{0,3},{1,0},{2,1},{3,2},{4,7},{5,4},{6,5},{7,6},{8,11},{9,8},{10,9... | collective-permute-start | bytes 3080 | tf_op jit(solution)/shard_map/ppermute | solution.py:234
  67.2 0.3 collective-permute-start.3
  67.5 1.4 %collective-permute-start.2 = (f32[8,32]{1,0:T(8,128)S(1)}, f32[8,32]{1,0:T(8,128)S(1)}, u32[]{:S(2)}, u32[]{:S(2)}) collective-permute-start(f32[8,32]{1,0:T(8,128)S(1)} %maxima.1), channel_id=1, source_target_pairs={{0,1},{1,2},{2,3},{3,0},{4,5},{5,6},{6,7},{7,4},{8,9},{9,10},{10,1... | collective-permute-start | bytes 3080 | tf_op jit(solution)/shard_map/ppermute | solution.py:234
  68.9 1.2 %merge.1 = bf16[128,1024]{1,0:T(8,128)(2,1)} custom-call(bf16[128,2176]{1,0:T(8,128)(2,1)S(1)} %reshape.21.got_ref.tail_ref), custom_call_target="tpu_custom_call" | custom-call | flops 100000000 | bytes 10000000 | tf_op jit(solution)/shard_map/merge/pallas_call | solution.py:237
  70.1 0.0 collective-permute-done.4
  70.1 0.0 collective-permute-done.3
  70.1 0.0 collective-permute-done.2
  70.1 0.6 add_bitcast_fusion
  (1 shorter events, 0.0 us)
Async XLA Ops:
  0.6 15.3 %copy-start = (bf16[128,1024]{1,0:T(8,128)(2,1)S(1)}, bf16[128,1024]{1,0:T(8,128)(2,1)}, u32[]{:S(2)}) copy-start(bf16[128,1024]{1,0:T(8,128)(2,1)} %q0_ref.1) | copy-start | bytes 786436
  0.6 23.5 %copy-start.1 = (s32[64,128]{1,0:T(8,128)S(1)}, s32[64,128]{1,0:T(8,128)}, u32[]{:S(2)}) copy-start(s32[64,128]{1,0:T(8,128)} %source_ref.1) | copy-start | bytes 98308
  0.7 23.5 %copy-start.2 = (s32[8]{0:T(128)S(1)}, s32[8]{0:T(128)}, u32[]{:S(2)}) copy-start(s32[8]{0:T(128)} %lengths_ref.1) | copy-start | bytes 100
  1.5 5.3 %collective-permute-start.1 = (bf16[128,256]{1,0:T(8,128)(2,1)S(1)}, bf16[128,256]{1,0:T(8,128)(2,1)S(1)}, u32[]{:S(2)}, u32[]{:S(2)}) collective-permute-start(bf16[128,256]{1,0:T(8,128)(2,1)S(1)} %pad_add_fusion.own_ref), channel_id=1, source_target_pairs={{0,32},{4,36},{8,40},{12,44},{16,48},{20,52},{24,56},{28,60},{32,6... | collective-permute-start | bytes 196616 | tf_op jit(solution)/shard_map/ppermute | solution.py:193
  7.7 24.1 %all-to-all-start = ((bf16[8,128,256]{2,1,0:T(8,128)(2,1)}), bf16[8,128,256]{2,1,0:T(8,128)(2,1)S(1)}, u32[]{:S(2)}, u32[]{:S(2)}) async-start(bf16[8,128,256]{2,1,0:T(8,128)(2,1)} %broadcast_select_fusion), calls=%async_computation | async-start | bytes 1048576 | tf_op jit(solution)/shard_map/all_to_all | solution.py:188
  15.9 8.2 %collective-permute-start = (bf16[128,1024]{1,0:T(8,128)(2,1)S(1)}, bf16[128,1024]{1,0:T(8,128)(2,1)S(1)}, u32[]{:S(2)}, u32[]{:S(2)}) collective-permute-start(bf16[128,1024]{1,0:T(8,128)(2,1)S(1)} %copy-done), channel_id=1, source_target_pairs={{32,0},{36,4},{40,8},{44,12},{48,16},{52,20},{56,24},{60,28},{64,3... | collective-permute-start | bytes 786440 | tf_op jit(solution)/shard_map/ppermute | solution.py:194
  62.0 8.1 %collective-permute-start.4 = (f32[8,32]{1,0:T(8,128)S(1)}, f32[8,32]{1,0:T(8,128)S(1)}, u32[]{:S(2)}, u32[]{:S(2)}) collective-permute-start(f32[8,32]{1,0:T(8,128)S(1)} %maxima.1), channel_id=1, source_target_pairs={{0,3},{1,0},{2,1},{3,2},{4,7},{5,4},{6,5},{7,6},{8,11},{9,8},{10,9... | collective-permute-start | bytes 3080 | tf_op jit(solution)/shard_map/ppermute | solution.py:234
  67.2 2.9 %collective-permute-start.3 = (f32[8,32]{1,0:T(8,128)S(1)}, f32[8,32]{1,0:T(8,128)S(1)}, u32[]{:S(2)}, u32[]{:S(2)}) collective-permute-start(f32[8,32]{1,0:T(8,128)S(1)} %maxima.1), channel_id=1, source_target_pairs={{0,2},{1,3},{2,0},{3,1},{4,6},{5,7},{6,4},{7,5},{8,10},{9,11},{10,... | collective-permute-start | bytes 3080 | tf_op jit(solution)/shard_map/ppermute | solution.py:234
  67.5 2.6 %collective-permute-start.2 = (f32[8,32]{1,0:T(8,128)S(1)}, f32[8,32]{1,0:T(8,128)S(1)}, u32[]{:S(2)}, u32[]{:S(2)}) collective-permute-start(f32[8,32]{1,0:T(8,128)S(1)} %maxima.1), channel_id=1, source_target_pairs={{0,1},{1,2},{2,3},{3,0},{4,5},{5,6},{6,7},{7,4},{8,9},{9,10},{10,1... | collective-permute-start | bytes 3080 | tf_op jit(solution)/shard_map/ppermute | solution.py:234

commit v6 on v5

--- a/solution.py
+++ b/solution.py
@@ -23,6 +23,7 @@
 SCALE = 1.0 / math.sqrt(HD)
 SCALE_LOG2E = SCALE * math.log2(math.e)
 HEADS_AT_ONCE = 2
+ORDER = tuple(range(RINGS))
 SPAN = GROUPS * HEADS
 
 
@@ -42,6 +43,10 @@
 
 def iota(shape, dim):
     return lax.broadcasted_iota(jnp.int32, shape, dim)
+
+
+def device_at(place):
+    return place % RINGS * RING + place // RINGS
 
 
 def prepare_kernel(
@@ -51,7 +56,7 @@
     lane = iota((ROWS, 128), 1)
     row = iota((ROWS, 128), 0)
     local = as_bf16(source_ref[...] - iota((CTX, 128), 1) // 2 * ROWS)
-    spread = as_bf16(iota((ROWS, CTX), 0) // 2 == iota((ROWS, CTX), 1))
+    spread = as_bf16(device_at(iota((ROWS, CTX), 0) // 2) == iota((ROWS, CTX), 1))
     table = jnp.dot(spread, local, preferred_element_type=jnp.float32)
     in_ring = me % RING
     base = me - in_ring
@@ -160,19 +165,26 @@
 
 def merge_kernel(got_ref, out_ref):
     row = iota((ROWS, 128), 0)
-    tail = got_ref[:, PARTS * WIDE :].astype(jnp.float32)
-
-    whole = tail + (pltpu.roll(tail, 128 - 8, 1) + pltpu.roll(tail, 128 - 16, 1))
-    shift = 2 * RING
-    far = pltpu.roll(pltpu.roll(whole, 128 - 24, 1), shift, 0)
-    share = 1.0 / (1.0 + jnp.exp(far - whole))
-    share = jnp.where(row < shift, 1.0, share)
+
+    to = iota((ROWS, ROWS), 0)
+    source = to // 2 % RING * 2 * RINGS + to // (2 * RING) * 2 + to % 2
+    from_near = as_bf16(iota((ROWS, ROWS), 1) == source)
+    from_far = as_bf16(iota((ROWS, ROWS), 1) == source - 2)
+    whole = jnp.concatenate([got_ref[:, :WIDE], got_ref[:, PARTS * WIDE :]], axis=1)
+    near = jnp.dot(from_near, whole, preferred_element_type=jnp.float32)
+    whole = jnp.concatenate([got_ref[:, WIDE : PARTS * WIDE], got_ref[:, PARTS * WIDE :]], axis=1)
+    far = jnp.dot(from_far, whole, preferred_element_type=jnp.float32)
+
+    def summed(tail):
+        return tail + (pltpu.roll(tail, 128 - 8, 1) + pltpu.roll(tail, 128 - 16, 1))
+
+    log_far = pltpu.roll(summed(far[:, WIDE:]), 128 - 24, 1)
+    share = 1.0 / (1.0 + jnp.exp(log_far - summed(near[:, WIDE:])))
+    share = jnp.where(row < 2 * RING, 1.0, share)
     for h in range(HEADS):
         w = share[:, h : h + 1]
-        mine = got_ref[:, h * HD : (h + 1) * HD].astype(jnp.float32)
-        other = got_ref[:, WIDE + h * HD : WIDE + (h + 1) * HD].astype(jnp.float32)
-        other = pltpu.roll(other, shift, 0)
-        out_ref[:, h * HD : (h + 1) * HD] = (mine * w + other * (1.0 - w)).astype(jnp.bfloat16)
+        at = slice(h * HD, (h + 1) * HD)
+        out_ref[:, at] = (near[:, at] * w + far[:, at] * (1.0 - w)).astype(jnp.bfloat16)
 
 
 VMEM = pl.BlockSpec(memory_space=pltpu.VMEM)
@@ -218,7 +230,12 @@
         name="attend",
     )(q_rows, bias, doc, window, own)
     got = lax.all_to_all(
-        sent.reshape(CTX, 2, wide), "ctx", split_axis=0, concat_axis=0, tiled=True
+        sent.reshape(CTX, 2, wide),
+        "ctx",
+        split_axis=0,
+        concat_axis=0,
+        tiled=True,
+        axis_index_groups=[[r * RING + z for z in range(RING) for r in ORDER]],
     )
     got = got.reshape(ROWS, wide)
     maxima = pl.pallas_call(

time: 70.9 us -> 70.1 us (0.989)
  blocking collectives: 25.9 us -> 24.4 us
    all_to_all x1, blocking collectives: 25.9 us -> 24.4 us  [body(): lax.all_to_all(sent.reshape(CTX, 2, wide), 'ctx', split_axis=0, concat_ax...]
  transfers between devices with their start and end apart: 6 -> 6, of which waited for: 3 -> 3; matrix products, arithmetic and copies ran while one was open for 0% -> 0% of each run, Pallas kernels for 3% -> 4%
where the time goes in v6:
time: 70.1 us; the launch traced here: 69.9 us
  blocking collectives  24.4 us (35%)
  starting transfers between devices  20.7 us (30%)
  waiting for transfers between devices  14.6 us (21%)
  Pallas kernels  6.57 us (9%)
  other arithmetic  2.32 us (3%)
  between operations  0.73 us (1%)
    all_to_all x1, blocking collectives, body(): lax.all_to_all(sent.reshape(CTX, 2, wide), 'ctx', split_axis=0, concat_ax...  24.4 us
    all_to_all x1, starting transfers between devices, exchange(): lax.all_to_all(x, 'ctx', split_axis=0, concat_axis=0, tiled=True, axis_in...  8.19 us
    ppermute x3, starting transfers between devices, body(): lax.ppermute(maxima, 'head', [(i, (i + k) % GROUPS) for i in range(GROUPS)])  7.24 us
    ppermute x1, waiting for transfers between devices, body(): lax.ppermute(queries, 'ctx', [(c + RING, c) for c in range(CTX - RING)])  6.9 us
    all_to_all x1, waiting for transfers between devices, exchange(): lax.all_to_all(x, 'ctx', split_axis=0, concat_axis=0, tiled=True, axis_in...  6.45 us
    ppermute x1, starting transfers between devices, body(): lax.ppermute(own, 'ctx', [(c, c + RING) for c in range(CTX - RING)])  4.03 us
    pallas_call x1, Pallas kernels, body(): pl.pallas_call(attend_kernel, out_shape=jax.ShapeDtypeStruct((ROWS, wide)...  3.62 us
    pallas_call x1, Pallas kernels, body(): pl.pallas_call(merge_kernel, out_shape=jax.ShapeDtypeStruct((ROWS, WIDE),...  1.52 us
  transfers between devices with their start and end apart: 6, of which 3 were waited for; matrix products, arithmetic and copies ran while one was open for 0% of the time, Pallas kernels for 4%

profile of v6, /device:TPU:1, one launch (start us, length us, event | category | flops | bytes accessed | tf_op | source)
XLA Modules:
  0.0 69.9 jit_solution(10523336532051675962)
XLA Ops:
  0.6 0.0 copy-start
  0.6 0.0 copy-start.1
  0.7 0.0 copy-start.2
  0.7 0.8 %pad_add_fusion.own_ref = bf16[128,256]{1,0:T(8,128)(2,1)S(1)} fusion(bf16[128,128]{1,0:T(8,128)(2,1)} %param.7, bf16[128,128]{1,0:T(8,128)(2,1)} %param.6), kind=kLoop, calls=%fused_computation.1 | loop fusion | flops 131072 | bytes 131072 | tf_op jit(solution)/shard_map/add | solution.py:204
  1.5 4.0 %collective-permute-start.1 = (bf16[128,256]{1,0:T(8,128)(2,1)S(1)}, bf16[128,256]{1,0:T(8,128)(2,1)S(1)}, u32[]{:S(2)}, u32[]{:S(2)}) collective-permute-start(bf16[128,256]{1,0:T(8,128)(2,1)S(1)} %pad_add_fusion.own_ref), channel_id=1, source_target_pairs={{0,32},{4,36},{8,40},{12,44},{16,48},{20,52},{24,56},{28,60},{32,6... | collective-permute-start | bytes 196616 | tf_op jit(solution)/shard_map/ppermute | solution.py:205
  5.5 1.3 %collective-permute-done.1 = bf16[128,256]{1,0:T(8,128)(2,1)S(1)} collective-permute-done((bf16[128,256]{1,0:T(8,128)(2,1)S(1)}, bf16[128,256]{1,0:T(8,128)(2,1)S(1)}, u32[]{:S(2)}, u32[]{:S(2)}) %collective-permute-start.1) | collective-permute-done | bytes 65568 | tf_op jit(solution)/shard_map/ppermute | solution.py:205
  6.8 0.9 %broadcast_select_fusion = bf16[8,128,256]{2,1,0:T(8,128)(2,1)} fusion(pred[8]{0:T(512)(128)(4,1)S(1)} %iota_compare_fusion, bf16[128,256]{1,0:T(8,128)(2,1)S(1)} %collective-permute-done.1, bf16[128,256]{1,0:T(8,128)(2,1)S(1)} %pad_add_fusion.own_ref), kind=kLoop, calls=%fused_computation | loop fusion | flops 262144 | bytes 655368 | tf_op jit(solution)/shard_map/jit(_where)/select_n | solution.py:208
  7.7 8.2 %all-to-all-start = ((bf16[8,128,256]{2,1,0:T(8,128)(2,1)}), bf16[8,128,256]{2,1,0:T(8,128)(2,1)S(1)}, u32[]{:S(2)}, u32[]{:S(2)}) async-start(bf16[8,128,256]{2,1,0:T(8,128)(2,1)} %broadcast_select_fusion), calls=%async_computation | async-start | bytes 1048576 | tf_op jit(solution)/shard_map/all_to_all | solution.py:200
  15.9 0.0 copy-done
  15.9 1.3 %collective-permute-start = (bf16[128,1024]{1,0:T(8,128)(2,1)S(1)}, bf16[128,1024]{1,0:T(8,128)(2,1)S(1)}, u32[]{:S(2)}, u32[]{:S(2)}) collective-permute-start(bf16[128,1024]{1,0:T(8,128)(2,1)S(1)} %copy-done), channel_id=1, source_target_pairs={{32,0},{36,4},{40,8},{44,12},{48,16},{52,20},{56,24},{60,28},{64,3... | collective-permute-start | bytes 786440 | tf_op jit(solution)/shard_map/ppermute | solution.py:206
  17.2 6.9 %collective-permute-done.q1_ref = bf16[128,1024]{1,0:T(8,128)(2,1)S(1)} collective-permute-done((bf16[128,1024]{1,0:T(8,128)(2,1)S(1)}, bf16[128,1024]{1,0:T(8,128)(2,1)S(1)}, u32[]{:S(2)}, u32[]{:S(2)}) %collective-permute-start) | collective-permute-done | bytes 262176 | tf_op jit(solution)/shard_map/ppermute | solution.py:206
  24.1 0.0 copy-done.1
  24.1 0.0 copy-done.2
  24.1 1.3 %prepare.1 = (bf16[2,1024,128]{2,1,0:T(8,128)(2,1)S(1)}, f32[2,128,1152]{2,1,0:T(8,128)S(1)}, s32[2,128,128]{2,1,0:T(8,128)S(1)}) custom-call(s32[8]{0:T(128)S(1)} %copy-done.2, s32[64,128]{1,0:T(8,128)S(1)} %copy-done.1, bf16[128,1024]{1,0:T(8,128)(2,1)S(1)} %copy-done, bf16[128,1024]{1,0:T(8,128)(2,1)S(1)} %collective-permute-done.q1_ref), custom_call_target="tpu_custom_call" | custom-call | tf_op jit(solution)/shard_map/prepare/pallas_call | solution.py:210
  25.4 6.4 %all-to-all-done = bf16[8,128,256]{2,1,0:T(8,128)(2,1)S(1)} async-done(((bf16[8,128,256]{2,1,0:T(8,128)(2,1)}), bf16[8,128,256]{2,1,0:T(8,128)(2,1)S(1)}, u32[]{:S(2)}, u32[]{:S(2)}) %all-to-all-start) | async-done | bytes 524320 | tf_op jit(solution)/shard_map/all_to_all | solution.py:200
  31.9 3.6 %attend.1 = bf16[128,2176]{1,0:T(8,128)(2,1)S(1)} custom-call(bf16[2,1024,128]{2,1,0:T(8,128)(2,1)S(1)} %get-tuple-element.5.q_ref, f32[2,128,1152]{2,1,0:T(8,128)S(1)} %get-tuple-element.6.bias_ref, s32[2,128,128]{2,1,0:T(8,128)S(1)} %get-tuple-element.7.doc_ref, bf16[1024,256]{1,0:T(8,128)(2,1)S(1)} %bitcast.3, bf16[128,256]{1,0:T(8,128)(2,1)S(1)} %pad_add_fusion.own_ref), custom_call_target="tpu_custom_call" | custom-call | tf_op jit(solution)/shard_map/attend/pallas_call | solution.py:223
  35.5 0.2 reshape.20
  35.7 24.4 %all_to_all.10 = bf16[64,2,2176]{2,1,0:T(2,128)(2,1)S(1)} all-to-all(bf16[64,2,2176]{2,1,0:T(2,128)(2,1)S(1)} %reshape.20), channel_id=1, replica_groups={{0,32,64,96,128,160,192,224,4,36,68,100,132,164,196,228,8,40,72,104,136..., dimensions={0} | all-to-all | bytes 1114112 | tf_op jit(solution)/shard_map/all_to_all | solution.py:232
  60.1 0.2 reshape.21.got_ref.tail_ref
  60.4 0.2 maxima.1
  60.5 5.5 %collective-permute-start.4 = (f32[8,32]{1,0:T(8,128)S(1)}, f32[8,32]{1,0:T(8,128)S(1)}, u32[]{:S(2)}, u32[]{:S(2)}) collective-permute-start(f32[8,32]{1,0:T(8,128)S(1)} %maxima.1), channel_id=1, source_target_pairs={{0,3},{1,0},{2,1},{3,2},{4,7},{5,4},{6,5},{7,6},{8,11},{9,8},{10,9... | collective-permute-start | bytes 3080 | tf_op jit(solution)/shard_map/ppermute | solution.py:251
  66.1 0.3 collective-permute-start.3
  66.4 1.4 %collective-permute-start.2 = (f32[8,32]{1,0:T(8,128)S(1)}, f32[8,32]{1,0:T(8,128)S(1)}, u32[]{:S(2)}, u32[]{:S(2)}) collective-permute-start(f32[8,32]{1,0:T(8,128)S(1)} %maxima.1), channel_id=1, source_target_pairs={{0,1},{1,2},{2,3},{3,0},{4,5},{5,6},{6,7},{7,4},{8,9},{9,10},{10,1... | collective-permute-start | bytes 3080 | tf_op jit(solution)/shard_map/ppermute | solution.py:251
  67.8 1.5 %merge.1 = bf16[128,1024]{1,0:T(8,128)(2,1)} custom-call(bf16[128,2176]{1,0:T(8,128)(2,1)S(1)} %reshape.21.got_ref.tail_ref), custom_call_target="tpu_custom_call" | custom-call | flops 100000000 | bytes 10000000 | tf_op jit(solution)/shard_map/merge/pallas_call | solution.py:254
  69.3 0.0 collective-permute-done.4
  69.3 0.0 collective-permute-done.3
  69.3 0.0 collective-permute-done.2
  69.3 0.6 add_bitcast_fusion
  (1 shorter events, 0.0 us)
Async XLA Ops:
  0.6 15.3 %copy-start = (bf16[128,1024]{1,0:T(8,128)(2,1)S(1)}, bf16[128,1024]{1,0:T(8,128)(2,1)}, u32[]{:S(2)}) copy-start(bf16[128,1024]{1,0:T(8,128)(2,1)} %q0_ref.1) | copy-start | bytes 786436
  0.6 23.5 %copy-start.1 = (s32[64,128]{1,0:T(8,128)S(1)}, s32[64,128]{1,0:T(8,128)}, u32[]{:S(2)}) copy-start(s32[64,128]{1,0:T(8,128)} %source_ref.1) | copy-start | bytes 98308
  0.7 23.5 %copy-start.2 = (s32[8]{0:T(128)S(1)}, s32[8]{0:T(128)}, u32[]{:S(2)}) copy-start(s32[8]{0:T(128)} %lengths_ref.1) | copy-start | bytes 100
  1.5 5.3 %collective-permute-start.1 = (bf16[128,256]{1,0:T(8,128)(2,1)S(1)}, bf16[128,256]{1,0:T(8,128)(2,1)S(1)}, u32[]{:S(2)}, u32[]{:S(2)}) collective-permute-start(bf16[128,256]{1,0:T(8,128)(2,1)S(1)} %pad_add_fusion.own_ref), channel_id=1, source_target_pairs={{0,32},{4,36},{8,40},{12,44},{16,48},{20,52},{24,56},{28,60},{32,6... | collective-permute-start | bytes 196616 | tf_op jit(solution)/shard_map/ppermute | solution.py:205
  7.7 24.1 %all-to-all-start = ((bf16[8,128,256]{2,1,0:T(8,128)(2,1)}), bf16[8,128,256]{2,1,0:T(8,128)(2,1)S(1)}, u32[]{:S(2)}, u32[]{:S(2)}) async-start(bf16[8,128,256]{2,1,0:T(8,128)(2,1)} %broadcast_select_fusion), calls=%async_computation | async-start | bytes 1048576 | tf_op jit(solution)/shard_map/all_to_all | solution.py:200
  15.9 8.2 %collective-permute-start = (bf16[128,1024]{1,0:T(8,128)(2,1)S(1)}, bf16[128,1024]{1,0:T(8,128)(2,1)S(1)}, u32[]{:S(2)}, u32[]{:S(2)}) collective-permute-start(bf16[128,1024]{1,0:T(8,128)(2,1)S(1)} %copy-done), channel_id=1, source_target_pairs={{32,0},{36,4},{40,8},{44,12},{48,16},{52,20},{56,24},{60,28},{64,3... | collective-permute-start | bytes 786440 | tf_op jit(solution)/shard_map/ppermute | solution.py:206
  60.5 8.8 %collective-permute-start.4 = (f32[8,32]{1,0:T(8,128)S(1)}, f32[8,32]{1,0:T(8,128)S(1)}, u32[]{:S(2)}, u32[]{:S(2)}) collective-permute-start(f32[8,32]{1,0:T(8,128)S(1)} %maxima.1), channel_id=1, source_target_pairs={{0,3},{1,0},{2,1},{3,2},{4,7},{5,4},{6,5},{7,6},{8,11},{9,8},{10,9... | collective-permute-start | bytes 3080 | tf_op jit(solution)/shard_map/ppermute | solution.py:251
  66.1 3.2 %collective-permute-start.3 = (f32[8,32]{1,0:T(8,128)S(1)}, f32[8,32]{1,0:T(8,128)S(1)}, u32[]{:S(2)}, u32[]{:S(2)}) collective-permute-start(f32[8,32]{1,0:T(8,128)S(1)} %maxima.1), channel_id=1, source_target_pairs={{0,2},{1,3},{2,0},{3,1},{4,6},{5,7},{6,4},{7,5},{8,10},{9,11},{10,... | collective-permute-start | bytes 3080 | tf_op jit(solution)/shard_map/ppermute | solution.py:251
  66.4 2.9 %collective-permute-start.2 = (f32[8,32]{1,0:T(8,128)S(1)}, f32[8,32]{1,0:T(8,128)S(1)}, u32[]{:S(2)}, u32[]{:S(2)}) collective-permute-start(f32[8,32]{1,0:T(8,128)S(1)} %maxima.1), channel_id=1, source_target_pairs={{0,1},{1,2},{2,3},{3,0},{4,5},{5,6},{6,7},{7,4},{8,9},{9,10},{10,1... | collective-permute-start | bytes 3080 | tf_op jit(solution)/shard_map/ppermute | solution.py:251

commit v7 on v6

--- a/solution.py
+++ b/solution.py
@@ -170,21 +170,28 @@
     source = to // 2 % RING * 2 * RINGS + to // (2 * RING) * 2 + to % 2
     from_near = as_bf16(iota((ROWS, ROWS), 1) == source)
     from_far = as_bf16(iota((ROWS, ROWS), 1) == source - 2)
-    whole = jnp.concatenate([got_ref[:, :WIDE], got_ref[:, PARTS * WIDE :]], axis=1)
-    near = jnp.dot(from_near, whole, preferred_element_type=jnp.float32)
-    whole = jnp.concatenate([got_ref[:, WIDE : PARTS * WIDE], got_ref[:, PARTS * WIDE :]], axis=1)
-    far = jnp.dot(from_far, whole, preferred_element_type=jnp.float32)
+
+    def ordered(rows, low, high):
+        return jnp.dot(rows, got_ref[:, low:high], preferred_element_type=jnp.float32)
+
+    tails = [ordered(rows, PARTS * WIDE, PARTS * WIDE + 128) for rows in (from_near, from_far)]
 
     def summed(tail):
         return tail + (pltpu.roll(tail, 128 - 8, 1) + pltpu.roll(tail, 128 - 16, 1))
 
-    log_far = pltpu.roll(summed(far[:, WIDE:]), 128 - 24, 1)
-    share = 1.0 / (1.0 + jnp.exp(log_far - summed(near[:, WIDE:])))
+    log_far = pltpu.roll(summed(tails[1]), 128 - 24, 1)
+    share = 1.0 / (1.0 + jnp.exp(log_far - summed(tails[0])))
     share = jnp.where(row < 2 * RING, 1.0, share)
-    for h in range(HEADS):
-        w = share[:, h : h + 1]
-        at = slice(h * HD, (h + 1) * HD)
-        out_ref[:, at] = (near[:, at] * w + far[:, at] * (1.0 - w)).astype(jnp.bfloat16)
+    for h in range(0, HEADS, 2):
+        low, high = h * HD, (h + 2) * HD
+        near = ordered(from_near, low, high)
+        far = ordered(from_far, WIDE + low, WIDE + high)
+        for k in range(2):
+            w = share[:, h + k : h + k + 1]
+            at = slice(k * HD, (k + 1) * HD)
+            out_ref[:, low + k * HD : low + (k + 1) * HD] = (
+                near[:, at] * w + far[:, at] * (1.0 - w)
+            ).astype(jnp.bfloat16)
 
 
 VMEM = pl.BlockSpec(memory_space=pltpu.VMEM)

time: 70.1 us -> 70 us (level)
  no operation moved by 1% of the time
where the time goes in v7:
time: 70 us; the launch traced here: 69.7 us
  blocking collectives  24.4 us (35%)
  starting transfers between devices  20.7 us (30%)
  waiting for transfers between devices  14.6 us (21%)
  Pallas kernels  6.44 us (9%)
  other arithmetic  2.32 us (3%)
  between operations  0.73 us (1%)
    all_to_all x1, blocking collectives, body(): lax.all_to_all(sent.reshape(CTX, 2, wide), 'ctx', split_axis=0, concat_ax...  24.4 us
    all_to_all x1, starting transfers between devices, exchange(): lax.all_to_all(x, 'ctx', split_axis=0, concat_axis=0, tiled=True, axis_in...  8.19 us
    ppermute x3, starting transfers between devices, body(): lax.ppermute(maxima, 'head', [(i, (i + k) % GROUPS) for i in range(GROUPS)])  7.24 us
    ppermute x1, waiting for transfers between devices, body(): lax.ppermute(queries, 'ctx', [(c + RING, c) for c in range(CTX - RING)])  6.9 us
    all_to_all x1, waiting for transfers between devices, exchange(): lax.all_to_all(x, 'ctx', split_axis=0, concat_axis=0, tiled=True, axis_in...  6.45 us
    ppermute x1, starting transfers between devices, body(): lax.ppermute(own, 'ctx', [(c, c + RING) for c in range(CTX - RING)])  4.03 us
    pallas_call x1, Pallas kernels, body(): pl.pallas_call(attend_kernel, out_shape=jax.ShapeDtypeStruct((ROWS, wide)...  3.62 us
  transfers between devices with their start and end apart: 6, of which 3 were waited for; matrix products, arithmetic and copies ran while one was open for 0% of the time, Pallas kernels for 4%

profile of v7, /device:TPU:1, one launch (start us, length us, event | category | flops | bytes accessed | tf_op | source)
XLA Modules:
  0.0 69.7 jit_solution(13969156945128339510)
XLA Ops:
  0.6 0.0 copy-start
  0.6 0.0 copy-start.1
  0.7 0.0 copy-start.2
  0.7 0.8 %pad_add_fusion.own_ref = bf16[128,256]{1,0:T(8,128)(2,1)S(1)} fusion(bf16[128,128]{1,0:T(8,128)(2,1)} %param.7, bf16[128,128]{1,0:T(8,128)(2,1)} %param.6), kind=kLoop, calls=%fused_computation.1 | loop fusion | flops 131072 | bytes 131072 | tf_op jit(solution)/shard_map/add | solution.py:211
  1.5 4.0 %collective-permute-start.1 = (bf16[128,256]{1,0:T(8,128)(2,1)S(1)}, bf16[128,256]{1,0:T(8,128)(2,1)S(1)}, u32[]{:S(2)}, u32[]{:S(2)}) collective-permute-start(bf16[128,256]{1,0:T(8,128)(2,1)S(1)} %pad_add_fusion.own_ref), channel_id=1, source_target_pairs={{0,32},{4,36},{8,40},{12,44},{16,48},{20,52},{24,56},{28,60},{32,6... | collective-permute-start | bytes 196616 | tf_op jit(solution)/shard_map/ppermute | solution.py:212
  5.5 1.3 %collective-permute-done.1 = bf16[128,256]{1,0:T(8,128)(2,1)S(1)} collective-permute-done((bf16[128,256]{1,0:T(8,128)(2,1)S(1)}, bf16[128,256]{1,0:T(8,128)(2,1)S(1)}, u32[]{:S(2)}, u32[]{:S(2)}) %collective-permute-start.1) | collective-permute-done | bytes 65568 | tf_op jit(solution)/shard_map/ppermute | solution.py:212
  6.8 0.9 %broadcast_select_fusion = bf16[8,128,256]{2,1,0:T(8,128)(2,1)} fusion(pred[8]{0:T(512)(128)(4,1)S(1)} %iota_compare_fusion, bf16[128,256]{1,0:T(8,128)(2,1)S(1)} %collective-permute-done.1, bf16[128,256]{1,0:T(8,128)(2,1)S(1)} %pad_add_fusion.own_ref), kind=kLoop, calls=%fused_computation | loop fusion | flops 262144 | bytes 655368 | tf_op jit(solution)/shard_map/jit(_where)/select_n | solution.py:215
  7.7 8.2 %all-to-all-start = ((bf16[8,128,256]{2,1,0:T(8,128)(2,1)}), bf16[8,128,256]{2,1,0:T(8,128)(2,1)S(1)}, u32[]{:S(2)}, u32[]{:S(2)}) async-start(bf16[8,128,256]{2,1,0:T(8,128)(2,1)} %broadcast_select_fusion), calls=%async_computation | async-start | bytes 1048576 | tf_op jit(solution)/shard_map/all_to_all | solution.py:207
  15.9 0.0 copy-done
  15.9 1.3 %collective-permute-start = (bf16[128,1024]{1,0:T(8,128)(2,1)S(1)}, bf16[128,1024]{1,0:T(8,128)(2,1)S(1)}, u32[]{:S(2)}, u32[]{:S(2)}) collective-permute-start(bf16[128,1024]{1,0:T(8,128)(2,1)S(1)} %copy-done), channel_id=1, source_target_pairs={{32,0},{36,4},{40,8},{44,12},{48,16},{52,20},{56,24},{60,28},{64,3... | collective-permute-start | bytes 786440 | tf_op jit(solution)/shard_map/ppermute | solution.py:213
  17.2 6.9 %collective-permute-done.q1_ref = bf16[128,1024]{1,0:T(8,128)(2,1)S(1)} collective-permute-done((bf16[128,1024]{1,0:T(8,128)(2,1)S(1)}, bf16[128,1024]{1,0:T(8,128)(2,1)S(1)}, u32[]{:S(2)}, u32[]{:S(2)}) %collective-permute-start) | collective-permute-done | bytes 262176 | tf_op jit(solution)/shard_map/ppermute | solution.py:213
  24.1 0.0 copy-done.1
  24.1 0.0 copy-done.2
  24.1 1.3 %prepare.1 = (bf16[2,1024,128]{2,1,0:T(8,128)(2,1)S(1)}, f32[2,128,1152]{2,1,0:T(8,128)S(1)}, s32[2,128,128]{2,1,0:T(8,128)S(1)}) custom-call(s32[8]{0:T(128)S(1)} %copy-done.2, s32[64,128]{1,0:T(8,128)S(1)} %copy-done.1, bf16[128,1024]{1,0:T(8,128)(2,1)S(1)} %copy-done, bf16[128,1024]{1,0:T(8,128)(2,1)S(1)} %collective-permute-done.q1_ref), custom_call_target="tpu_custom_call" | custom-call | tf_op jit(solution)/shard_map/prepare/pallas_call | solution.py:217
  25.4 6.4 %all-to-all-done = bf16[8,128,256]{2,1,0:T(8,128)(2,1)S(1)} async-done(((bf16[8,128,256]{2,1,0:T(8,128)(2,1)}), bf16[8,128,256]{2,1,0:T(8,128)(2,1)S(1)}, u32[]{:S(2)}, u32[]{:S(2)}) %all-to-all-start) | async-done | bytes 524320 | tf_op jit(solution)/shard_map/all_to_all | solution.py:207
  31.9 3.6 %attend.1 = bf16[128,2176]{1,0:T(8,128)(2,1)S(1)} custom-call(bf16[2,1024,128]{2,1,0:T(8,128)(2,1)S(1)} %get-tuple-element.5.q_ref, f32[2,128,1152]{2,1,0:T(8,128)S(1)} %get-tuple-element.6.bias_ref, s32[2,128,128]{2,1,0:T(8,128)S(1)} %get-tuple-element.7.doc_ref, bf16[1024,256]{1,0:T(8,128)(2,1)S(1)} %bitcast.3, bf16[128,256]{1,0:T(8,128)(2,1)S(1)} %pad_add_fusion.own_ref), custom_call_target="tpu_custom_call" | custom-call | tf_op jit(solution)/shard_map/attend/pallas_call | solution.py:230
  35.5 0.2 reshape.20
  35.7 24.4 %all_to_all.10 = bf16[64,2,2176]{2,1,0:T(2,128)(2,1)S(1)} all-to-all(bf16[64,2,2176]{2,1,0:T(2,128)(2,1)S(1)} %reshape.20), channel_id=1, replica_groups={{0,32,64,96,128,160,192,224,4,36,68,100,132,164,196,228,8,40,72,104,136..., dimensions={0} | all-to-all | bytes 1114112 | tf_op jit(solution)/shard_map/all_to_all | solution.py:239
  60.1 0.2 reshape.21.got_ref.tail_ref
  60.4 0.2 maxima.1
  60.5 5.5 %collective-permute-start.4 = (f32[8,32]{1,0:T(8,128)S(1)}, f32[8,32]{1,0:T(8,128)S(1)}, u32[]{:S(2)}, u32[]{:S(2)}) collective-permute-start(f32[8,32]{1,0:T(8,128)S(1)} %maxima.1), channel_id=1, source_target_pairs={{0,3},{1,0},{2,1},{3,2},{4,7},{5,4},{6,5},{7,6},{8,11},{9,8},{10,9... | collective-permute-start | bytes 3080 | tf_op jit(solution)/shard_map/ppermute | solution.py:258
  66.1 0.3 collective-permute-start.3
  66.4 1.4 %collective-permute-start.2 = (f32[8,32]{1,0:T(8,128)S(1)}, f32[8,32]{1,0:T(8,128)S(1)}, u32[]{:S(2)}, u32[]{:S(2)}) collective-permute-start(f32[8,32]{1,0:T(8,128)S(1)} %maxima.1), channel_id=1, source_target_pairs={{0,1},{1,2},{2,3},{3,0},{4,5},{5,6},{6,7},{7,4},{8,9},{9,10},{10,1... | collective-permute-start | bytes 3080 | tf_op jit(solution)/shard_map/ppermute | solution.py:258
  67.8 1.4 %merge.1 = bf16[128,1024]{1,0:T(8,128)(2,1)} custom-call(bf16[128,2176]{1,0:T(8,128)(2,1)S(1)} %reshape.21.got_ref.tail_ref), custom_call_target="tpu_custom_call" | custom-call | flops 100000000 | bytes 10000000 | tf_op jit(solution)/shard_map/merge/pallas_call | solution.py:261
  69.1 0.0 collective-permute-done.4
  69.1 0.0 collective-permute-done.3
  69.1 0.0 collective-permute-done.2
  69.1 0.6 add_bitcast_fusion
  (1 shorter events, 0.0 us)
Async XLA Ops:
  0.6 15.3 %copy-start = (bf16[128,1024]{1,0:T(8,128)(2,1)S(1)}, bf16[128,1024]{1,0:T(8,128)(2,1)}, u32[]{:S(2)}) copy-start(bf16[128,1024]{1,0:T(8,128)(2,1)} %q0_ref.1) | copy-start | bytes 786436
  0.6 23.5 %copy-start.1 = (s32[64,128]{1,0:T(8,128)S(1)}, s32[64,128]{1,0:T(8,128)}, u32[]{:S(2)}) copy-start(s32[64,128]{1,0:T(8,128)} %source_ref.1) | copy-start | bytes 98308
  0.7 23.5 %copy-start.2 = (s32[8]{0:T(128)S(1)}, s32[8]{0:T(128)}, u32[]{:S(2)}) copy-start(s32[8]{0:T(128)} %lengths_ref.1) | copy-start | bytes 100
  1.5 5.3 %collective-permute-start.1 = (bf16[128,256]{1,0:T(8,128)(2,1)S(1)}, bf16[128,256]{1,0:T(8,128)(2,1)S(1)}, u32[]{:S(2)}, u32[]{:S(2)}) collective-permute-start(bf16[128,256]{1,0:T(8,128)(2,1)S(1)} %pad_add_fusion.own_ref), channel_id=1, source_target_pairs={{0,32},{4,36},{8,40},{12,44},{16,48},{20,52},{24,56},{28,60},{32,6... | collective-permute-start | bytes 196616 | tf_op jit(solution)/shard_map/ppermute | solution.py:212
  7.7 24.1 %all-to-all-start = ((bf16[8,128,256]{2,1,0:T(8,128)(2,1)}), bf16[8,128,256]{2,1,0:T(8,128)(2,1)S(1)}, u32[]{:S(2)}, u32[]{:S(2)}) async-start(bf16[8,128,256]{2,1,0:T(8,128)(2,1)} %broadcast_select_fusion), calls=%async_computation | async-start | bytes 1048576 | tf_op jit(solution)/shard_map/all_to_all | solution.py:207
  15.9 8.2 %collective-permute-start = (bf16[128,1024]{1,0:T(8,128)(2,1)S(1)}, bf16[128,1024]{1,0:T(8,128)(2,1)S(1)}, u32[]{:S(2)}, u32[]{:S(2)}) collective-permute-start(bf16[128,1024]{1,0:T(8,128)(2,1)S(1)} %copy-done), channel_id=1, source_target_pairs={{32,0},{36,4},{40,8},{44,12},{48,16},{52,20},{56,24},{60,28},{64,3... | collective-permute-start | bytes 786440 | tf_op jit(solution)/shard_map/ppermute | solution.py:213
  60.5 8.6 %collective-permute-start.4 = (f32[8,32]{1,0:T(8,128)S(1)}, f32[8,32]{1,0:T(8,128)S(1)}, u32[]{:S(2)}, u32[]{:S(2)}) collective-permute-start(f32[8,32]{1,0:T(8,128)S(1)} %maxima.1), channel_id=1, source_target_pairs={{0,3},{1,0},{2,1},{3,2},{4,7},{5,4},{6,5},{7,6},{8,11},{9,8},{10,9... | collective-permute-start | bytes 3080 | tf_op jit(solution)/shard_map/ppermute | solution.py:258
  66.1 3.1 %collective-permute-start.3 = (f32[8,32]{1,0:T(8,128)S(1)}, f32[8,32]{1,0:T(8,128)S(1)}, u32[]{:S(2)}, u32[]{:S(2)}) collective-permute-start(f32[8,32]{1,0:T(8,128)S(1)} %maxima.1), channel_id=1, source_target_pairs={{0,2},{1,3},{2,0},{3,1},{4,6},{5,7},{6,4},{7,5},{8,10},{9,11},{10,... | collective-permute-start | bytes 3080 | tf_op jit(solution)/shard_map/ppermute | solution.py:258
  66.4 2.8 %collective-permute-start.2 = (f32[8,32]{1,0:T(8,128)S(1)}, f32[8,32]{1,0:T(8,128)S(1)}, u32[]{:S(2)}, u32[]{:S(2)}) collective-permute-start(f32[8,32]{1,0:T(8,128)S(1)} %maxima.1), channel_id=1, source_target_pairs={{0,1},{1,2},{2,3},{3,0},{4,5},{5,6},{6,7},{7,4},{8,9},{9,10},{10,1... | collective-permute-start | bytes 3080 | tf_op jit(solution)/shard_map/ppermute | solution.py:258
